TPU v7x, 512 devices: a whole 4x4x16 slice. The times are simulated.
512 devices in a mesh: grp: 8 (over z_lo, core), shard: 64 (over z_hi, y, x).
Axes of the slice: x: 4, y: 4, z: 16 (z_hi: 4, z_lo: 4; z = z_hi * 4 + z_lo), core: 2. Of those that a mesh axis runs over, the one named last changes fastest.
Arguments:
- out_param: float32 [8, 256, 16384], P('grp', 'shard'), may hold values from -0.12 to 0.12
- out_grad: bfloat16 [8, 256, 16384], P('grp', 'shard'), may hold values from -2000 to 2000
- out_first: float32 [8, 256, 16384], P('grp', 'shard'), may hold values from -50 to 50
- out_second: float32 [8, 256, 16384], P('grp', 'shard'), may hold values from 0 to 6200
- pair_param: float32 [8, 256, 2048], P('grp', 'shard'), may hold values from -0.12 to 0.12
- pair_grad: bfloat16 [8, 256, 2048], P('grp', 'shard'), may hold values from -2000 to 2000
- pair_first: float32 [8, 256, 2048], P('grp', 'shard'), may hold values from -50 to 50
- pair_second: float32 [8, 256, 2048], P('grp', 'shard'), may hold values from 0 to 6200
Outputs:
- updated_out: float32 [8, 256, 16384], P('grp', 'shard')
- first_out: float32 [8, 256, 16384], P('grp', 'shard')
- second_out: float32 [8, 256, 16384], P('grp', 'shard')
- serving_out: bfloat16 [8, 256, 16384], P(None, None, 'shard')
- updated_pair: float32 [8, 256, 2048], P('grp', 'shard')
- first_pair: float32 [8, 256, 2048], P('grp', 'shard')
- second_pair: float32 [8, 256, 2048], P('grp', 'shard')
- serving_pair: bfloat16 [8, 256, 16384], P(None, None, 'shard')
All inputs are finite; a program needn't handle non-finite values.
Results may differ from a plain program's by a relative error of at most 0.001.
Values may be sent and summed in bfloat16 or wider, within the bound.
No kernel may reach another device: no remote copies, remote signals or barrier semaphores. Data moves between devices by JAX's collectives and lax.ppermute only.
A program may use at most 64 MiB of HBM per device.

v0:
```python
import jax
import jax.numpy as jnp
from jax import lax
from jax.sharding import PartitionSpec as P

KV_HEADS = 8
HD = 128


def apply_update(param, gradient, first, second, factor):
    scaled = gradient.astype(jnp.float32) * factor
    first_new = 0.9 * first + 0.1 * scaled
    second_new = 0.95 * second + 0.05 * scaled * scaled
    corr_first = 1.0 - 0.9**20
    corr_second = 1.0 - 0.95**20
    step_size = first_new / corr_first / (jnp.sqrt(second_new / corr_second) + 1e-08)
    param_new = param - 0.001 * (step_size + 0.1 * param)
    return (param_new, first_new, second_new, param_new.astype(jnp.bfloat16))


def head_layout(pair_narrow, copy_count):
    layer_count, row_count, column_count = pair_narrow.shape
    split_heads = pair_narrow.reshape(layer_count, row_count, 2, KV_HEADS, HD)
    by_head = jnp.transpose(split_heads, (0, 1, 3, 2, 4)).reshape(
        layer_count, row_count, KV_HEADS, 2 * HD
    )
    copied = jnp.broadcast_to(
        by_head[:, :, :, None, :], (layer_count, row_count, KV_HEADS, copy_count, 2 * HD)
    )
    return copied.reshape(layer_count, row_count, KV_HEADS * copy_count * 2 * HD)


def per_device(
    out_param, out_grad, out_first, out_second, pair_param, pair_grad, pair_first, pair_second
):
    out_wide = out_grad.astype(jnp.float32)
    pair_wide = pair_grad.astype(jnp.float32)
    local_squares = jnp.sum(out_wide * out_wide) + jnp.sum(pair_wide * pair_wide)
    summed = lax.psum(local_squares, ("grp", "shard"))
    count = lax.axis_size("grp") * lax.axis_size("shard") * (out_grad.size + pair_grad.size)
    factor = jnp.minimum(1.0, 1.5 * jnp.sqrt(jnp.float32(count)) / jnp.sqrt(summed))
    out_res = apply_update(out_param, out_grad, out_first, out_second, factor)
    pair_res = apply_update(pair_param, pair_grad, pair_first, pair_second, factor)
    copy_count = lax.axis_size("shard") // KV_HEADS
    gathered = (
        lax.all_gather(out_res[3], "grp", axis=0, tiled=True),
        lax.all_gather(pair_res[3], "grp", axis=0, tiled=True),
    )
    expanded = head_layout(gathered[1], copy_count)
    serving = (
        lax.all_to_all(gathered[0], "shard", split_axis=2, concat_axis=1, tiled=True),
        lax.all_to_all(expanded, "shard", split_axis=2, concat_axis=1, tiled=True),
    )
    return (
        out_res[0],
        out_res[1],
        out_res[2],
        serving[0],
        pair_res[0],
        pair_res[1],
        pair_res[2],
        serving[1],
    )


def solution(mesh):
    placed = (
        P("grp", "shard", None),
        P("grp", "shard", None),
        P("grp", "shard", None),
        P("grp", "shard", None),
        P("grp", "shard", None),
        P("grp", "shard", None),
        P("grp", "shard", None),
        P("grp", "shard", None),
    )
    return jax.shard_map(
        per_device,
        mesh=mesh,
        in_specs=placed,
        out_specs=(
            P("grp", "shard", None),
            P("grp", "shard", None),
            P("grp", "shard", None),
            P(None, None, "shard"),
            P("grp", "shard", None),
            P("grp", "shard", None),
            P("grp", "shard", None),
            P(None, None, "shard"),
        ),
        check_vma=False,
    )
```

profile of v0, /device:TPU:1, one launch (start us, length us, event | category | flops | bytes accessed | tf_op | source)
XLA Modules:
  0.0 393.8 jit_solution(13425826012293036518)
XLA Ops:
  7.2 1.6 fusion.2
  8.8 1.3 fusion.6
  11.4 111.0 %psum.7 = f32[]{:T(128)} all-reduce(f32[]{:T(128)S(6)} %add.35), channel_id=1, replica_groups=mesh['grp'=8,'shard'=64] {'grp','shard'}, use_global_device_ids=true, to_apply=%region_2.0 | all-reduce | flops 1 | bytes 8 | tf_op jit(solution)/shard_map/psum | solution.py:39
  123.1 1.5 fusion.8
  124.6 14.6 %all_gather.7 = bf16[8,4,2048]{2,1,0:T(4,128)(2,1)S(1)} all-gather(bf16[1,4,2048]{2,1,0:T(4,128)(2,1)S(1)} %get-tuple-element.8), channel_id=1, replica_groups=mesh['grp'=8,'shard'=64] {'grp'}, dimensions={0}, use_global_device_ids=true | all-gather | bytes 147456 | tf_op jit(solution)/shard_map/all_gather | solution.py:47
  139.3 0.1 reshape.23
  139.3 1.1 copy.26
  140.5 0.0 copy-start
  140.5 0.0 copy-start.1
  140.5 0.0 copy-start.2
  140.5 0.0 copy-start.3
  140.5 6.1 %broadcast_in_dim.8 = bf16[8,4,8,8,256]{0,1,4,3,2:T(4,128)(2,1)} broadcast(bf16[8,4,8,256]{0,1,3,2:T(4,128)(2,1)S(1)} %copy.26), dimensions={0,1,2,4} | broadcast | bytes 1179648 | tf_op jit(solution)/shard_map/broadcast_in_dim | solution.py:27
  146.7 20.7 %reshape.27 = bf16[64,2,4096]{2,1,0:T(2,128)(2,1)} reshape(bf16[16384,4,8]{2,1,0:T(4,128)(2,1)} %bitcast.14) | data formatting | bytes 2097152
  167.3 8.8 %all-to-all-start.1 = ((bf16[64,2,4096]{2,1,0:T(2,128)(2,1)}), bf16[64,2,4096]{2,1,0:T(2,128)(2,1)S(1)}, u32[]{:S(2)}, u32[]{:S(2)}) async-start(bf16[64,2,4096]{2,1,0:T(2,128)(2,1)} %reshape.27), calls=%async_computation.1 | async-start | bytes 2097152 | tf_op jit(solution)/shard_map/all_to_all | solution.py:52
  176.1 0.0 all-gather.2.cloned.1.call-start
  176.2 0.0 copy-done
  176.2 0.0 copy-done.1
  176.2 0.0 copy-done.2
  176.2 1.3 fusion.11
  177.5 0.0 all-gather.2.cloned.1.call-update
  177.6 56.9 %all-gather.2.cloned.1.call-done = bf16[8,4,16384]{2,1,0:T(4,128)(2,1)} async-done(((bf16[1,4,16384]{2,1,0:T(4,128)(2,1)}), bf16[8,4,16384]{2,1,0:T(4,128)(2,1)}) %all-gather.2.cloned.1.call-update) | async-done | bytes 1048592 | tf_op jit(solution)/shard_map/all_gather | solution.py:46
  234.5 19.8 %copy.24 = bf16[8,4,16384]{0,1,2:T(4,128)(2,1)} copy(bf16[8,4,16384]{2,1,0:T(4,128)(2,1)} %all-gather.2.cloned.1.call-done) | data formatting | bytes 2097152 | tf_op jit(solution)/shard_map/all_gather | solution.py:46
  254.3 20.7 %reshape.25 = bf16[64,2,4096]{2,1,0:T(2,128)(2,1)} reshape(bf16[16384,4,8]{2,1,0:T(4,128)(2,1)} %bitcast.15) | data formatting | bytes 2097152
  274.9 0.0 all-to-all-done.1
  274.9 16.8 %all-to-all-start = ((bf16[64,2,4096]{2,1,0:T(2,128)(2,1)}), bf16[64,2,4096]{2,1,0:T(2,128)(2,1)S(1)}, u32[]{:S(2)}, u32[]{:S(2)}) async-start(bf16[64,2,4096]{2,1,0:T(2,128)(2,1)} %reshape.25), calls=%async_computation | async-start | bytes 2097152 | tf_op jit(solution)/shard_map/all_to_all | solution.py:51
  291.7 20.8 %reshape.28 = bf16[16384,4,8]{2,1,0:T(4,128)(2,1)} reshape(bf16[64,2,4096]{2,1,0:T(2,128)(2,1)S(1)} %all-to-all-done.1) | data formatting | bytes 2097152
  312.5 20.9 %copy.27 = bf16[8,64,4,256]{3,2,1,0:T(4,128)(2,1)S(1)} copy(bf16[8,64,4,256]{0,2,3,1:T(4,128)(2,1)} %bitcast.16) | data formatting | bytes 2097152 | tf_op jit(solution)/shard_map/all_to_all | solution.py:52
  333.4 1.1 all_to_all.33
  334.5 9.8 %all-to-all-done = bf16[64,2,4096]{2,1,0:T(2,128)(2,1)S(1)} async-done(((bf16[64,2,4096]{2,1,0:T(2,128)(2,1)}), bf16[64,2,4096]{2,1,0:T(2,128)(2,1)S(1)}, u32[]{:S(2)}, u32[]{:S(2)}) %all-to-all-start) | async-done | bytes 1048608 | tf_op jit(solution)/shard_map/all_to_all | solution.py:51
  344.2 20.8 %reshape.26 = bf16[16384,4,8]{2,1,0:T(4,128)(2,1)} reshape(bf16[64,2,4096]{2,1,0:T(2,128)(2,1)S(1)} %all-to-all-done) | data formatting | bytes 2097152
  365.0 20.9 %copy.25 = bf16[8,64,4,256]{3,2,1,0:T(4,128)(2,1)S(1)} copy(bf16[8,64,4,256]{0,2,3,1:T(4,128)(2,1)} %bitcast.17) | data formatting | bytes 2097152 | tf_op jit(solution)/shard_map/all_to_all | solution.py:51
  385.9 1.1 all_to_all.29
  (1 shorter events, 0.0 us)
Async XLA Ops:
  140.5 35.7 %copy-start = (bf16[1,4,16384]{2,1,0:T(4,128)(2,1)S(1)}, bf16[1,4,16384]{2,1,0:T(4,128)(2,1)}, u32[]{:S(2)}) copy-start(bf16[1,4,16384]{2,1,0:T(4,128)(2,1)} %param.9) | copy-start | bytes 393220
  140.5 35.7 %copy-start.1 = (f32[1,4,16384]{2,1,0:T(4,128)S(1)}, f32[1,4,16384]{2,1,0:T(4,128)}, u32[]{:S(2)}) copy-start(f32[1,4,16384]{2,1,0:T(4,128)} %param.8) | copy-start | bytes 786436
  140.5 35.7 %copy-start.2 = (f32[1,4,16384]{2,1,0:T(4,128)S(1)}, f32[1,4,16384]{2,1,0:T(4,128)}, u32[]{:S(2)}) copy-start(f32[1,4,16384]{2,1,0:T(4,128)} %param.10) | copy-start | bytes 786436
  140.5 35.7 %copy-start.3 = (f32[1,4,16384]{2,1,0:T(4,128)S(1)}, f32[1,4,16384]{2,1,0:T(4,128)}, u32[]{:S(2)}) copy-start(f32[1,4,16384]{2,1,0:T(4,128)} %param.11) | copy-start | bytes 786436
  167.3 107.6 %all-to-all-start.1 = ((bf16[64,2,4096]{2,1,0:T(2,128)(2,1)}), bf16[64,2,4096]{2,1,0:T(2,128)(2,1)S(1)}, u32[]{:S(2)}, u32[]{:S(2)}) async-start(bf16[64,2,4096]{2,1,0:T(2,128)(2,1)} %reshape.27), calls=%async_computation.1 | async-start | bytes 2097152 | tf_op jit(solution)/shard_map/all_to_all | solution.py:52
  176.1 58.3 %all-gather.2.cloned.1.call-start = ((), (), s32[]{:S(2)}) async-start(), calls=%async_computation.2 | async-start | bytes 1179648 | tf_op jit(solution)/shard_map/all_gather | solution.py:46
  274.9 69.3 %all-to-all-start = ((bf16[64,2,4096]{2,1,0:T(2,128)(2,1)}), bf16[64,2,4096]{2,1,0:T(2,128)(2,1)S(1)}, u32[]{:S(2)}, u32[]{:S(2)}) async-start(bf16[64,2,4096]{2,1,0:T(2,128)(2,1)} %reshape.25), calls=%async_computation | async-start | bytes 2097152 | tf_op jit(solution)/shard_map/all_to_all | solution.py:51
Sparse Core Ops, SparseCore 0:
  179.6 54.8 all-gather.1
where the time goes:
time: 399 us; the launch traced here: 394 us
  local copies, waits for them, and re-layouts  154 us (39%)
  blocking collectives  126 us (32%)
  waiting for transfers between devices  66.7 us (17%)
  starting transfers between devices  25.6 us (6%)
  between operations  16.1 us (4%)
  other arithmetic  5.8 us (1%)
    psum x1, blocking collectives, per_device(): summed = lax.psum(local_squares, ('grp', 'shard'))  111 us
    unnamed x12, local copies, waits for them, and re-layouts  82.9 us
    all_gather x1, waiting for transfers between devices, per_device(): lax.all_gather(out_res[3], 'grp', axis=0, tiled=True)  56.9 us
    all_to_all x2, local copies, waits for them, and re-layouts, per_device(): lax.all_to_all(gathered[0], 'shard', split_axis=2, concat_axis=1, tiled=T...  22 us
    all_to_all x2, local copies, waits for them, and re-layouts, per_device(): lax.all_to_all(expanded, 'shard', split_axis=2, concat_axis=1, tiled=True)  22 us
    all_gather x1, local copies, waits for them, and re-layouts, per_device(): lax.all_gather(out_res[3], 'grp', axis=0, tiled=True)  19.8 us
    all_to_all x1, starting transfers between devices, per_device(): lax.all_to_all(gathered[0], 'shard', split_axis=2, concat_axis=1, tiled=T...  16.8 us
    all_gather x1, blocking collectives, per_device(): lax.all_gather(pair_res[3], 'grp', axis=0, tiled=True)  14.6 us
  transfers between devices with their start and end apart: 3, of which 2 were waited for; matrix products, arithmetic and copies ran while one was open for 21% of the time, Pallas kernels for 0%

commit v1 on v0

v1 whole, which is shorter than its diff:
```python
import numpy as np
import jax
import jax.numpy as jnp
from jax import lax
from jax.experimental import pallas as pl
from jax.experimental.pallas import tpu as pltpu
from jax.sharding import Mesh
from jax.sharding import PartitionSpec as P

KV_HEADS = 8
HD = 128
GROUP = ("zl", "core")
SHARD = ("zh", "y", "x")
RING = ("zh", "zl", "core")
PLANE = ("y", "x")


def apply_update(param, gradient, first, second, factor):
    scaled = gradient.astype(jnp.float32) * factor
    first_new = 0.9 * first + 0.1 * scaled
    second_new = 0.95 * second + 0.05 * scaled * scaled
    corr_first = 1.0 - 0.9**20
    corr_second = 1.0 - 0.95**20
    step_size = first_new / corr_first / (jnp.sqrt(second_new / corr_second) + 1e-08)
    param_new = param - 0.001 * (step_size + 0.1 * param)
    return (param_new, first_new, second_new, param_new.astype(jnp.bfloat16))


def total_over(value, axes):
    members = lax.axis_size(axes)
    copies = jnp.broadcast_to(value.reshape(1, 1, 1), (members, 1, 128))
    received = lax.all_to_all(copies, axes, split_axis=0, concat_axis=0, tiled=True)
    return jnp.sum(received[:, 0, 0])


def place_kernel(where_ref, *refs):
    blocks, (out_ref, pair_ref), sems = refs[:8], refs[8:10], refs[10]
    copies = []
    for i in range(8):
        layer = where_ref[i]
        copies.append(pltpu.make_async_copy(blocks[i].at[0], out_ref.at[layer], sems.at[i, 0]))
        copies.append(pltpu.make_async_copy(blocks[i].at[1], pair_ref.at[layer], sems.at[i, 1]))
    for copy in copies:
        copy.start()
    for copy in copies:
        copy.wait()


def place(where, blocks):
    _, rows, columns = blocks[0].shape
    shape = jax.ShapeDtypeStruct((8, rows, columns), jnp.bfloat16)
    anywhere, held = pl.BlockSpec(memory_space=pl.ANY), pl.BlockSpec(memory_space=pltpu.VMEM)
    return pl.pallas_call(
        place_kernel,
        out_shape=(shape, shape),
        in_specs=[pl.BlockSpec(memory_space=pltpu.SMEM)] + [held] * 8,
        out_specs=(anywhere, anywhere),
        scratch_shapes=[pltpu.SemaphoreType.DMA((8, 2))],
    )(where, *blocks)


def per_device(
    out_param, out_grad, out_first, out_second, pair_param, pair_grad, pair_first, pair_second
):
    out_wide = out_grad.astype(jnp.float32)
    pair_wide = pair_grad.astype(jnp.float32)
    local_squares = jnp.sum(out_wide * out_wide) + jnp.sum(pair_wide * pair_wide)
    summed = total_over(total_over(local_squares, RING), PLANE)
    groups, shards = lax.axis_size(GROUP), lax.axis_size(SHARD)
    count = groups * shards * (out_grad.size + pair_grad.size)
    factor = jnp.minimum(1.0, 1.5 * jnp.sqrt(jnp.float32(count)) / jnp.sqrt(summed))
    out_res = apply_update(out_param, out_grad, out_first, out_second, factor)
    pair_res = apply_update(pair_param, pair_grad, pair_first, pair_second, factor)

    rows = out_param.shape[1]
    width = out_param.shape[2] // shards
    out_blocks = jnp.transpose(out_res[3].reshape(rows, shards, width), (1, 0, 2))
    by_head = jnp.transpose(pair_res[3].reshape(rows, 2, KV_HEADS, HD), (2, 0, 1, 3))
    by_head = by_head.reshape(KV_HEADS, 1, rows, 2 * HD)
    pair_blocks = jnp.broadcast_to(by_head, (KV_HEADS, shards // KV_HEADS, rows, 2 * HD))
    pair_blocks = pair_blocks.reshape(shards, rows, 2 * HD)
    sent = jnp.stack([out_blocks, pair_blocks], axis=1)
    mine = lax.all_to_all(sent, SHARD, split_axis=0, concat_axis=0, tiled=True)
    mine = jnp.transpose(mine, (1, 0, 2, 3)).reshape(2, shards * rows, width)

    zl, core = lax.axis_index("zl"), lax.axis_index("core")
    blocks, where = [mine], [2 * zl + core]
    for k in range(1, 4):
        blocks.append(lax.ppermute(mine, "zl", [(i, i ^ k) for i in range(4)]))
        where.append(2 * (zl ^ k) + core)
    for k in range(4):
        blocks.append(lax.ppermute(blocks[k], "core", [(0, 1), (1, 0)]))
        where.append(2 * (zl ^ k) + (1 - core))
    serving = place(jnp.stack(where).astype(jnp.int32), blocks)
    return (
        out_res[0],
        out_res[1],
        out_res[2],
        serving[0],
        pair_res[0],
        pair_res[1],
        pair_res[2],
        serving[1],
    )


def solution(mesh):
    fine = Mesh(mesh.devices.reshape(4, 2, 4, 4, 4), ("zl", "core", "zh", "y", "x"))
    owned = P(GROUP, SHARD, None)
    served = P(None, None, SHARD)
    return jax.shard_map(
        per_device,
        mesh=fine,
        in_specs=(owned,) * 8,
        out_specs=(owned, owned, owned, served, owned, owned, owned, served),
        check_vma=False,
    )
```

time: 399 us -> 116 us (0.29); the launches traced: 394 us -> 115 us
  local copies, waits for them, and re-layouts: 154 us -> 2.39 us
  blocking collectives: 126 us -> 63.8 us
  waiting for transfers between devices: 66.7 us -> 9.36 us
  between operations: 16.1 us -> 2.96 us
    psum x1 -> x0, blocking collectives: 111 us -> none  [per_device(): summed = lax.psum(local_squares, ('grp', 'shard'))]
    unnamed x12 -> x29, local copies, waits for them, and re-layouts: 82.9 us -> 0.92 us
    all_to_all x0 -> x3, blocking collectives: none -> 63.8 us  [the longest x2 41.3 us: total_over(): lax.all_to_all(copies, axes, split_axis=0, concat_axis=0, tiled=True)]
    all_gather x1 -> x0, waiting for transfers between devices: 56.9 us -> none  [per_device(): lax.all_gather(out_res[3], 'grp', axis=0, tiled=True)]
    all_to_all x4 -> x0, local copies, waits for them, and re-layouts: 43.9 us -> none  [the longest x2 22 us: per_device(): lax.all_to_all(gathered[0], 'shard', split_axis=2, concat_axis=1, tiled=T...]
    ppermute x0 -> x7, starting transfers between devices: none -> 26.4 us  [the longest x4 14.2 us: per_device(): blocks.append(lax.ppermute(blocks[k], 'core', [(0, 1), (1, 0)]))]
    all_to_all x2 -> x0, starting transfers between devices: 25.6 us -> none  [the longest x1 16.8 us: per_device(): lax.all_to_all(gathered[0], 'shard', split_axis=2, concat_axis=1, tiled=T...]
    all_gather x1 -> x0, local copies, waits for them, and re-layouts: 19.8 us -> none  [per_device(): lax.all_gather(out_res[3], 'grp', axis=0, tiled=True)]
  transfers between devices with their start and end apart: 3 -> 7, of which waited for: 2 -> 2; matrix products, arithmetic and copies ran while one was open for 21% -> 0% of each run, Pallas kernels for 0% -> 0%
where the time goes in v1:
time: 116 us; the launch traced here: 115 us
  blocking collectives  63.8 us (55%)
  starting transfers between devices  26.4 us (23%)
  waiting for transfers between devices  9.36 us (8%)
  other arithmetic  7.42 us (6%)
  between operations  2.96 us (3%)
  Pallas kernels  2.95 us (3%)
  local copies, waits for them, and re-layouts  2.39 us (2%)
    all_to_all x2, blocking collectives, total_over(): lax.all_to_all(copies, axes, split_axis=0, concat_axis=0, tiled=True)  41.3 us
    all_to_all x1, blocking collectives, per_device(): mine = lax.all_to_all(sent, SHARD, split_axis=0, concat_axis=0, tiled=True)  22.5 us
    ppermute x4, starting transfers between devices, per_device(): blocks.append(lax.ppermute(blocks[k], 'core', [(0, 1), (1, 0)]))  14.2 us
    ppermute x3, starting transfers between devices, per_device(): blocks.append(lax.ppermute(mine, 'zl', [(i, i ^ k) for i in range(4)]))  12.2 us
    ppermute x3, waiting for transfers between devices, per_device(): blocks.append(lax.ppermute(mine, 'zl', [(i, i ^ k) for i in range(4)]))  8.48 us
    pallas_call x1, Pallas kernels, place(): pl.pallas_call(place_kernel, out_shape=(shape, shape), in_specs=[pl.Block...  2.95 us
  transfers between devices with their start and end apart: 7, of which 2 were waited for; matrix products, arithmetic and copies ran while one was open for 0% of the time, Pallas kernels for 0%

profile of v1, /device:TPU:1, one launch (start us, length us, event | category | flops | bytes accessed | tf_op | source)
XLA Modules:
  0.0 115.3 jit_solution(1960143528802911491)
XLA Ops:
  0.6 1.3 %fusion.6 = f32[]{:T(128)} fusion(bf16[1,4,2048]{2,1,0:T(4,128)(2,1)} %param.13), kind=kLoop, calls=%fused_computation.14 | loop fusion | flops 24575 | bytes 16388 | tf_op jit(solution)/shard_map/reduce_sum | solution.py:67
  2.0 1.7 %fusion.2 = f32[]{:T(128)} fusion(bf16[1,4,16384]{2,1,0:T(4,128)(2,1)} %param.9), kind=kLoop, calls=%fused_computation.5 | loop fusion | flops 196607 | bytes 131076 | tf_op jit(solution)/shard_map/reduce_sum | solution.py:67
  5.0 28.3 %all_to_all.15 = f32[32,1,128]{2,1,0:T(1,128)S(1)} all-to-all(f32[32,1,128]{2,1,0:T(1,128)S(1)} %broadcast_in_dim.8), channel_id=1, replica_groups=mesh['zl'=4,'core'=2,'zh'=4,'y'=4,'x'=4] {'zh','zl','core'}, dimensions={0} | all-to-all | bytes 32768 | tf_op jit(solution)/shard_map/all_to_all | solution.py:32
  33.4 0.6 slice_reduce_fusion
  34.0 0.6 broadcast_in_dim.18
  34.6 13.0 %all_to_all.16 = f32[16,1,128]{2,1,0:T(1,128)S(1)} all-to-all(f32[16,1,128]{2,1,0:T(1,128)S(1)} %broadcast_in_dim.18), channel_id=1, replica_groups=mesh['zl'=4,'core'=2,'zh'=4,'y'=4,'x'=4] {'y','x'}, dimensions={0} | all-to-all | bytes 16384 | tf_op jit(solution)/shard_map/all_to_all | solution.py:32
  47.6 0.6 slice_reduce_fusion.1
  49.0 0.0 copy-start.1
  49.0 0.7 convert_bitcast_fusion
  49.7 0.2 copy-done.1
  49.9 2.3 %fusion.8 = (bf16[1,4,16384]{2,1,0:T(4,128)(2,1)S(1)}, f32[1,4,16384]{2,1,0:T(4,128)}, f32[1,4,16384]{2,1,0:T(4,128)}, f32[1,4,16384]{2,1,0:T(4,128)}) fusion(f32[1,4,16384]{2,1,0:T(4,128)S(1)} %copy-done.9, f32[]{:T(128)S(6)} %min_shard_map.3, bf16[1,4,16384]{2,1,0:T(4,128)(2,1)S(1)} %copy-done.1, f32[1,4,16384]{2,1,0:T(4,128)} %param.10, ...), kind=kLoop, calls=%fused_computation.22 | loop fusion | flops 1179648 | bytes 1835012 | tf_op jit(solution)/shard_map/convert_element_type | solution.py:26
  52.2 0.2 pad_maximum_fusion
  52.4 22.5 %all_to_all.17 = bf16[64,2,4,256]{3,2,1,0:T(4,128)(2,1)S(1)} all-to-all(bf16[64,2,4,256]{3,2,1,0:T(4,128)(2,1)S(1)} %pad_maximum_fusion), channel_id=1, replica_groups=mesh['zl'=4,'core'=2,'zh'=4,'y'=4,'x'=4] {'zh','y','x'}, dimensions={0} | all-to-all | bytes 524288 | tf_op jit(solution)/shard_map/all_to_all | solution.py:83
  74.9 0.1 copy.30
  75.0 0.1 reshape.37.refs_0_
  75.1 7.0 %collective-permute-start.2 = (bf16[2,256,256]{2,1,0:T(8,128)(2,1)S(1)}, bf16[2,256,256]{2,1,0:T(8,128)(2,1)S(1)}, u32[]{:S(2)}, u32[]{:S(2)}) collective-permute-start(bf16[2,256,256]{2,1,0:T(8,128)(2,1)S(1)} %reshape.37.refs_0_), channel_id=1, source_target_pairs={{0,384},{128,256},{256,128},{384,0},{1,385},{129,257},{257,129},{3... | collective-permute-start | bytes 786440 | tf_op jit(solution)/shard_map/ppermute | solution.py:89
  82.1 3.0 %collective-permute-start.1 = (bf16[2,256,256]{2,1,0:T(8,128)(2,1)S(1)}, bf16[2,256,256]{2,1,0:T(8,128)(2,1)S(1)}, u32[]{:S(2)}, u32[]{:S(2)}) collective-permute-start(bf16[2,256,256]{2,1,0:T(8,128)(2,1)S(1)} %reshape.37.refs_0_), channel_id=1, source_target_pairs={{0,256},{128,384},{256,0},{384,128},{1,257},{129,385},{257,1},{385... | collective-permute-start | bytes 786440 | tf_op jit(solution)/shard_map/ppermute | solution.py:89
  85.1 2.2 %collective-permute-start = (bf16[2,256,256]{2,1,0:T(8,128)(2,1)S(1)}, bf16[2,256,256]{2,1,0:T(8,128)(2,1)S(1)}, u32[]{:S(2)}, u32[]{:S(2)}) collective-permute-start(bf16[2,256,256]{2,1,0:T(8,128)(2,1)S(1)} %reshape.37.refs_0_), channel_id=1, source_target_pairs={{0,128},{128,0},{256,384},{384,256},{1,129},{129,1},{257,385},{385... | collective-permute-start | bytes 786440 | tf_op jit(solution)/shard_map/ppermute | solution.py:89
  87.3 6.3 %collective-permute-start.3 = (bf16[2,256,256]{2,1,0:T(8,128)(2,1)S(1)}, bf16[2,256,256]{2,1,0:T(8,128)(2,1)S(1)}, u32[]{:S(2)}, u32[]{:S(2)}) collective-permute-start(bf16[2,256,256]{2,1,0:T(8,128)(2,1)S(1)} %reshape.37.refs_0_), channel_id=1, source_target_pairs={{0,64},{64,0},{1,65},{65,1},{2,66},{66,2},{3,67},{67,3},{4,68},{68... | collective-permute-start | bytes 786440 | tf_op jit(solution)/shard_map/ppermute | solution.py:92
  93.6 0.0 collective-permute-done.2.refs_3_
  93.6 1.9 %collective-permute-start.6 = (bf16[2,256,256]{2,1,0:T(8,128)(2,1)S(1)}, bf16[2,256,256]{2,1,0:T(8,128)(2,1)S(1)}, u32[]{:S(2)}, u32[]{:S(2)}) collective-permute-start(bf16[2,256,256]{2,1,0:T(8,128)(2,1)S(1)} %collective-permute-done.2.refs_3_), channel_id=1, source_target_pairs={{0,64},{64,0},{1,65},{65,1},{2,66},{66,2},{3,67},{67,3},{4,68},{68... | collective-permute-start | bytes 786440 | tf_op jit(solution)/shard_map/ppermute | solution.py:92
  95.5 8.5 %collective-permute-done.1.refs_2_ = bf16[2,256,256]{2,1,0:T(8,128)(2,1)S(1)} collective-permute-done((bf16[2,256,256]{2,1,0:T(8,128)(2,1)S(1)}, bf16[2,256,256]{2,1,0:T(8,128)(2,1)S(1)}, u32[]{:S(2)}, u32[]{:S(2)}) %collective-permute-start.1) | collective-permute-done | bytes 262176 | tf_op jit(solution)/shard_map/ppermute | solution.py:89
  104.0 4.1 %collective-permute-start.5 = (bf16[2,256,256]{2,1,0:T(8,128)(2,1)S(1)}, bf16[2,256,256]{2,1,0:T(8,128)(2,1)S(1)}, u32[]{:S(2)}, u32[]{:S(2)}) collective-permute-start(bf16[2,256,256]{2,1,0:T(8,128)(2,1)S(1)} %collective-permute-done.1.refs_2_), channel_id=1, source_target_pairs={{0,64},{64,0},{1,65},{65,1},{2,66},{66,2},{3,67},{67,3},{4,68},{68... | collective-permute-start | bytes 786440 | tf_op jit(solution)/shard_map/ppermute | solution.py:92
  108.1 0.0 collective-permute-done.refs_1_
  108.1 1.9 %collective-permute-start.4 = (bf16[2,256,256]{2,1,0:T(8,128)(2,1)S(1)}, bf16[2,256,256]{2,1,0:T(8,128)(2,1)S(1)}, u32[]{:S(2)}, u32[]{:S(2)}) collective-permute-start(bf16[2,256,256]{2,1,0:T(8,128)(2,1)S(1)} %collective-permute-done.refs_1_), channel_id=1, source_target_pairs={{0,64},{64,0},{1,65},{65,1},{2,66},{66,2},{3,67},{67,3},{4,68},{68... | collective-permute-start | bytes 786440 | tf_op jit(solution)/shard_map/ppermute | solution.py:92
  110.1 0.6 stack.41.where_ref
  110.7 0.0 collective-permute-done.3.refs_4_
  110.7 0.0 collective-permute-done.6.refs_7_
  110.7 0.0 collective-permute-done.5.refs_6_
  110.7 0.9 collective-permute-done.4.refs_5_
  111.6 0.7 copy-done.8
  112.3 3.0 %shard_map.143 = (bf16[8,256,256]{2,1,0:T(8,128)(2,1)}, bf16[8,256,256]{2,1,0:T(8,128)(2,1)}) custom-call(s32[8]{0:T(128)} %stack.41.where_ref, bf16[2,256,256]{2,1,0:T(8,128)(2,1)} %copy-done, bf16[2,256,256]{2,1,0:T(8,128)(2,1)} %copy-done.4, bf16[2,256,256]{2,1,0:T(8,128)(2,1)} %copy-done.3, bf16[2,256,256]{2,1,0:T(8,128)(2,1)} %copy-done.2, ...), custom_call_target="tpu_custom_call" | custom-call | tf_op jit(solution)/shard_map/pallas_call | solution.py:53
  (31 shorter events, 0.1 us)
Async XLA Ops:
  2.0 46.9 %copy-start.10 = (bf16[1,4,2048]{2,1,0:T(4,128)(2,1)S(1)}, bf16[1,4,2048]{2,1,0:T(4,128)(2,1)}, u32[]{:S(2)}) copy-start(bf16[1,4,2048]{2,1,0:T(4,128)(2,1)} %param.13) | copy-start | bytes 49156
  2.0 47.0 %copy-start.11 = (f32[1,4,2048]{2,1,0:T(4,128)S(1)}, f32[1,4,2048]{2,1,0:T(4,128)}, u32[]{:S(2)}) copy-start(f32[1,4,2048]{2,1,0:T(4,128)} %param.12) | copy-start | bytes 98308
  2.0 47.0 %copy-start.12 = (f32[1,4,2048]{2,1,0:T(4,128)S(1)}, f32[1,4,2048]{2,1,0:T(4,128)}, u32[]{:S(2)}) copy-start(f32[1,4,2048]{2,1,0:T(4,128)} %param.14) | copy-start | bytes 98308
  2.0 47.0 %copy-start.13 = (f32[1,4,2048]{2,1,0:T(4,128)S(1)}, f32[1,4,2048]{2,1,0:T(4,128)}, u32[]{:S(2)}) copy-start(f32[1,4,2048]{2,1,0:T(4,128)} %param.15) | copy-start | bytes 98308
  3.6 46.1 %copy-start.9 = (f32[1,4,16384]{2,1,0:T(4,128)S(1)}, f32[1,4,16384]{2,1,0:T(4,128)}, u32[]{:S(2)}) copy-start(f32[1,4,16384]{2,1,0:T(4,128)} %param.8) | copy-start | bytes 786436
  49.0 0.9 copy-start.1
  75.1 36.5 %copy-start = (bf16[2,256,256]{2,1,0:T(8,128)(2,1)}, bf16[2,256,256]{2,1,0:T(8,128)(2,1)S(1)}, u32[]{:S(2)}) copy-start(bf16[2,256,256]{2,1,0:T(8,128)(2,1)S(1)} %reshape.37.refs_0_) | copy-start | bytes 786436
  75.1 18.5 %collective-permute-start.2 = (bf16[2,256,256]{2,1,0:T(8,128)(2,1)S(1)}, bf16[2,256,256]{2,1,0:T(8,128)(2,1)S(1)}, u32[]{:S(2)}, u32[]{:S(2)}) collective-permute-start(bf16[2,256,256]{2,1,0:T(8,128)(2,1)S(1)} %reshape.37.refs_0_), channel_id=1, source_target_pairs={{0,384},{128,256},{256,128},{384,0},{1,385},{129,257},{257,129},{3... | collective-permute-start | bytes 786440 | tf_op jit(solution)/shard_map/ppermute | solution.py:89
  82.1 21.9 %collective-permute-start.1 = (bf16[2,256,256]{2,1,0:T(8,128)(2,1)S(1)}, bf16[2,256,256]{2,1,0:T(8,128)(2,1)S(1)}, u32[]{:S(2)}, u32[]{:S(2)}) collective-permute-start(bf16[2,256,256]{2,1,0:T(8,128)(2,1)S(1)} %reshape.37.refs_0_), channel_id=1, source_target_pairs={{0,256},{128,384},{256,0},{384,128},{1,257},{129,385},{257,1},{385... | collective-permute-start | bytes 786440 | tf_op jit(solution)/shard_map/ppermute | solution.py:89
  85.1 23.0 %collective-permute-start = (bf16[2,256,256]{2,1,0:T(8,128)(2,1)S(1)}, bf16[2,256,256]{2,1,0:T(8,128)(2,1)S(1)}, u32[]{:S(2)}, u32[]{:S(2)}) collective-permute-start(bf16[2,256,256]{2,1,0:T(8,128)(2,1)S(1)} %reshape.37.refs_0_), channel_id=1, source_target_pairs={{0,128},{128,0},{256,384},{384,256},{1,129},{129,1},{257,385},{385... | collective-permute-start | bytes 786440 | tf_op jit(solution)/shard_map/ppermute | solution.py:89
  87.3 23.4 %collective-permute-start.3 = (bf16[2,256,256]{2,1,0:T(8,128)(2,1)S(1)}, bf16[2,256,256]{2,1,0:T(8,128)(2,1)S(1)}, u32[]{:S(2)}, u32[]{:S(2)}) collective-permute-start(bf16[2,256,256]{2,1,0:T(8,128)(2,1)S(1)} %reshape.37.refs_0_), channel_id=1, source_target_pairs={{0,64},{64,0},{1,65},{65,1},{2,66},{66,2},{3,67},{67,3},{4,68},{68... | collective-permute-start | bytes 786440 | tf_op jit(solution)/shard_map/ppermute | solution.py:92
  93.6 18.0 %copy-start.2 = (bf16[2,256,256]{2,1,0:T(8,128)(2,1)}, bf16[2,256,256]{2,1,0:T(8,128)(2,1)S(1)}, u32[]{:S(2)}) copy-start(bf16[2,256,256]{2,1,0:T(8,128)(2,1)S(1)} %collective-permute-done.2.refs_3_) | copy-start | bytes 786436
  93.6 17.1 %collective-permute-start.6 = (bf16[2,256,256]{2,1,0:T(8,128)(2,1)S(1)}, bf16[2,256,256]{2,1,0:T(8,128)(2,1)S(1)}, u32[]{:S(2)}, u32[]{:S(2)}) collective-permute-start(bf16[2,256,256]{2,1,0:T(8,128)(2,1)S(1)} %collective-permute-done.2.refs_3_), channel_id=1, source_target_pairs={{0,64},{64,0},{1,65},{65,1},{2,66},{66,2},{3,67},{67,3},{4,68},{68... | collective-permute-start | bytes 786440 | tf_op jit(solution)/shard_map/ppermute | solution.py:92
  104.0 7.6 %copy-start.3 = (bf16[2,256,256]{2,1,0:T(8,128)(2,1)}, bf16[2,256,256]{2,1,0:T(8,128)(2,1)S(1)}, u32[]{:S(2)}) copy-start(bf16[2,256,256]{2,1,0:T(8,128)(2,1)S(1)} %collective-permute-done.1.refs_2_) | copy-start | bytes 786436
  104.0 6.7 %collective-permute-start.5 = (bf16[2,256,256]{2,1,0:T(8,128)(2,1)S(1)}, bf16[2,256,256]{2,1,0:T(8,128)(2,1)S(1)}, u32[]{:S(2)}, u32[]{:S(2)}) collective-permute-start(bf16[2,256,256]{2,1,0:T(8,128)(2,1)S(1)} %collective-permute-done.1.refs_2_), channel_id=1, source_target_pairs={{0,64},{64,0},{1,65},{65,1},{2,66},{66,2},{3,67},{67,3},{4,68},{68... | collective-permute-start | bytes 786440 | tf_op jit(solution)/shard_map/ppermute | solution.py:92
  108.1 3.5 %copy-start.4 = (bf16[2,256,256]{2,1,0:T(8,128)(2,1)}, bf16[2,256,256]{2,1,0:T(8,128)(2,1)S(1)}, u32[]{:S(2)}) copy-start(bf16[2,256,256]{2,1,0:T(8,128)(2,1)S(1)} %collective-permute-done.refs_1_) | copy-start | bytes 786436
  108.1 3.4 %collective-permute-start.4 = (bf16[2,256,256]{2,1,0:T(8,128)(2,1)S(1)}, bf16[2,256,256]{2,1,0:T(8,128)(2,1)S(1)}, u32[]{:S(2)}, u32[]{:S(2)}) collective-permute-start(bf16[2,256,256]{2,1,0:T(8,128)(2,1)S(1)} %collective-permute-done.refs_1_), channel_id=1, source_target_pairs={{0,64},{64,0},{1,65},{65,1},{2,66},{66,2},{3,67},{67,3},{4,68},{68... | collective-permute-start | bytes 786440 | tf_op jit(solution)/shard_map/ppermute | solution.py:92
  110.7 0.9 copy-start.5
  110.7 0.9 copy-start.6
  110.7 0.9 copy-start.7
  111.6 0.7 copy-start.8

commit v2 on v1

v2 whole, which is shorter than its diff:
```python
import jax
import jax.numpy as jnp
from jax import lax
from jax.experimental import pallas as pl
from jax.experimental.pallas import tpu as pltpu
from jax.sharding import Mesh
from jax.sharding import PartitionSpec as P

KV_HEADS = 8
HD = 128
LANES = 128
GROUP = ("zl", "core")
SHARD = ("zh", "y", "x")
RING = ("zh", "zl", "core")
PLANE = ("y", "x")
TURNS = (0, 2, 1, 3)
VMEM = pl.BlockSpec(memory_space=pltpu.VMEM)
ANY = pl.BlockSpec(memory_space=pl.ANY)
WIDE = pltpu.CompilerParams(vmem_limit_bytes=60 * 1024 * 1024)
SLIM = pltpu.CompilerParams(vmem_limit_bytes=8 * 1024 * 1024)


def apply_update(param, gradient, first, second, factor):
    scaled = gradient.astype(jnp.float32) * factor
    first_new = 0.9 * first + 0.1 * scaled
    second_new = 0.95 * second + 0.05 * scaled * scaled
    corr_first = 1.0 - 0.9**20
    corr_second = 1.0 - 0.95**20
    step_size = first_new / corr_first / (jnp.sqrt(second_new / corr_second) + 1e-08)
    param_new = param - 0.001 * (step_size + 0.1 * param)
    return (param_new, first_new, second_new)


def squares_kernel(out_ref, pair_ref, sums_ref):
    total = jnp.zeros((4, LANES), jnp.float32)
    for ref in (pair_ref, out_ref):
        for at in range(0, ref.shape[2], LANES):
            wide = ref[0, :, at : at + LANES].astype(jnp.float32)
            total = total + wide * wide
    row = jnp.sum(total, axis=0, keepdims=True)
    sums_ref[...] = jnp.broadcast_to(row[None], sums_ref.shape)


def add_kernel(got_ref, sums_ref):
    sums_ref[...] = jnp.broadcast_to(jnp.sum(got_ref[...], axis=0, keepdims=True), sums_ref.shape)


def send_kernel(count, *refs):
    got_ref, out_refs, pair_refs, (sent_ref, factor_ref) = refs[0], refs[1:5], refs[5:9], refs[9:]
    summed = jnp.sum(jnp.sum(got_ref[...], axis=0), keepdims=True)
    factor = jnp.minimum(1.0, 1.5 * jnp.sqrt(jnp.float32(count)) / jnp.sqrt(summed))
    factor_ref[...] = factor

    def narrow(refs, at, size):
        param, grad, first, second = [ref[0, :, at : at + size] for ref in refs]
        return apply_update(param, grad, first, second, factor)[0].astype(jnp.bfloat16)

    shards, _, _, width = sent_ref.shape
    for s in range(shards):
        sent_ref[s, 0] = narrow(out_refs, s * width, width)
    copies = shards // KV_HEADS
    for h in range(KV_HEADS):
        key = narrow(pair_refs, h * HD, HD)
        value = narrow(pair_refs, (KV_HEADS + h) * HD, HD)
        for s in range(h * copies, (h + 1) * copies):
            sent_ref[s, 1, :, :HD] = key
            sent_ref[s, 1, :, HD:] = value


def state_kernel(*refs):
    factor = refs[0][...]
    for given, made in ((refs[1:5], refs[9:12]), (refs[5:9], refs[12:15])):
        size = min(given[0].shape[2], 1024)
        for at in range(0, given[0].shape[2], size):
            values = apply_update(*[ref[0, :, at : at + size] for ref in given], factor)
            for ref, value in zip(made, values):
                ref[0, :, at : at + size] = value


def place_kernel(*refs):
    blocks, out_ref, pair_ref, sems = refs[:8], refs[8], refs[9], refs[10]
    zl, core = lax.axis_index("zl"), lax.axis_index("core")
    copies = []
    for i, ref in enumerate(blocks):
        layer = 2 * (zl ^ TURNS[i % 4]) + (core if i < 4 else 1 - core)
        copies.append(pltpu.make_async_copy(ref.at[0], out_ref.at[layer], sems.at[i, 0]))
        copies.append(pltpu.make_async_copy(ref.at[1], pair_ref.at[layer], sems.at[i, 1]))
    for copy in copies:
        copy.start()
    for copy in copies:
        copy.wait()


def swap(value, axes):
    return lax.all_to_all(value, axes, split_axis=0, concat_axis=0, tiled=True)


def per_device(*given):
    groups, shards = lax.axis_size(GROUP), lax.axis_size(SHARD)
    devices = groups * shards
    count = devices * (given[1].size + given[5].size)
    rows = given[0].shape[1]
    width = given[0].shape[2] // shards

    def sums(axes):
        return jax.ShapeDtypeStruct((lax.axis_size(axes), 1, LANES), jnp.float32)

    squares = pl.pallas_call(
        squares_kernel, out_shape=sums(RING), in_specs=[VMEM] * 2, out_specs=VMEM,
        compiler_params=WIDE,
    )(given[1], given[5])
    ring_sums = pl.pallas_call(
        add_kernel, out_shape=sums(PLANE), in_specs=[VMEM], out_specs=VMEM,
        compiler_params=SLIM,
    )(swap(squares, RING))
    plane_sums = swap(ring_sums, PLANE)
    sent, factor = pl.pallas_call(
        lambda *refs: send_kernel(count, *refs),
        out_shape=(
            jax.ShapeDtypeStruct((shards, 2, rows, width), jnp.bfloat16),
            jax.ShapeDtypeStruct((1, 1), jnp.float32),
        ),
        in_specs=[VMEM] * 9,
        out_specs=(VMEM, VMEM),
        compiler_params=WIDE,
    )(plane_sums, *given)
    mine = swap(sent, SHARD)

    mine, factor = lax.optimization_barrier((mine, factor))
    state = pl.pallas_call(
        state_kernel,
        out_shape=[
            jax.ShapeDtypeStruct(given[i].shape, jnp.float32) for i in (0, 0, 0, 4, 4, 4)
        ],
        in_specs=[VMEM] * 9,
        out_specs=[VMEM] * 6,
        compiler_params=WIDE,
        cost_estimate=pl.CostEstimate(
            flops=20 * count // devices, bytes_accessed=26 * count // devices, transcendentals=0
        ),
    )(factor, *given)

    mine = jnp.transpose(mine, (1, 0, 2, 3)).reshape(2, shards * rows, width)
    near = [mine]
    for k in TURNS[1:]:
        near.append(lax.ppermute(mine, "zl", [(i, i ^ k) for i in range(4)]))
    near[0], state = lax.optimization_barrier((near[0], state))
    far = [lax.ppermute(block, "core", [(0, 1), (1, 0)]) for block in near]
    serving_shape = jax.ShapeDtypeStruct((groups, shards * rows, width), jnp.bfloat16)
    serving = pl.pallas_call(
        place_kernel,
        out_shape=(serving_shape, serving_shape),
        in_specs=[ANY] * 8,
        out_specs=(ANY, ANY),
        scratch_shapes=[pltpu.SemaphoreType.DMA((8, 2))],
        compiler_params=SLIM,
    )(*near, *far)
    return (*state[:3], serving[0], *state[3:], serving[1])


def solution(mesh):
    fine = Mesh(mesh.devices.reshape(4, 2, 4, 4, 4), ("zl", "core", "zh", "y", "x"))
    owned = P(GROUP, SHARD, None)
    served = P(None, None, SHARD)
    return jax.shard_map(
        per_device,
        mesh=fine,
        in_specs=(owned,) * 8,
        out_specs=(owned, owned, owned, served, owned, owned, owned, served),
        check_vma=False,
    )
```

time: 116 us -> 105 us (0.905)
  other arithmetic: 7.42 us -> 0 us
  Pallas kernels: 2.95 us -> 8.47 us
  waiting for transfers between devices: 9.36 us -> 3.84 us
  local copies, waits for them, and re-layouts: 2.39 us -> 0.16 us
  between operations: 2.96 us -> 0.74 us
    pallas_call x1 -> x5, Pallas kernels: 2.95 us -> 8.47 us  [the longest x1 2.96 us: per_device(): pl.pallas_call(state_kernel, out_shape=[jax.ShapeDtypeStruct(given[i].sha...]
    ppermute x7, waiting for transfers between devices: 9.36 us -> 3.84 us  [the longest x3 2.73 us: per_device(): near.append(lax.ppermute(mine, 'zl', [(i, i ^ k) for i in range(4)]))]
    reduce_sum x4 -> x0, other arithmetic: 4.25 us -> none  [the longest x1 1.66 us: per_device(): jnp.sum(out_wide * out_wide) + jnp.sum(pair_wide * pair_wide)]
    convert_element_type x1 -> x0, other arithmetic: 2.31 us -> none  [apply_update(): return (param_new, first_new, second_new, param_new.astype(jnp.bfloat16))]
  transfers between devices with their start and end apart: 7 -> 7, of which waited for: 2 -> 2; matrix products, arithmetic and copies ran while one was open for 0% -> 0% of each run, Pallas kernels for 0% -> 3%
where the time goes in v2:
time: 105 us
  blocking collectives  64.6 us (62%)
  starting transfers between devices  26.8 us (26%)
  Pallas kernels  8.47 us (8%)
  waiting for transfers between devices  3.84 us (4%)
    all_to_all x3, blocking collectives, swap(): return lax.all_to_all(value, axes, split_axis=0, concat_axis=0, tiled=True)  64.6 us
    ppermute x4, starting transfers between devices, per_device(): far = [lax.ppermute(block, 'core', [(0, 1), (1, 0)]) for block in near]  15.1 us
    ppermute x3, starting transfers between devices, per_device(): near.append(lax.ppermute(mine, 'zl', [(i, i ^ k) for i in range(4)]))  11.8 us
    pallas_call x1, Pallas kernels, per_device(): pl.pallas_call(state_kernel, out_shape=[jax.ShapeDtypeStruct(given[i].sha...  2.96 us
    ppermute x3, waiting for transfers between devices, per_device(): near.append(lax.ppermute(mine, 'zl', [(i, i ^ k) for i in range(4)]))  2.73 us
    pallas_call x1, Pallas kernels, per_device(): pl.pallas_call(lambda *refs: send_kernel(count, *refs), out_shape=(jax.Sh...  2.36 us
  transfers between devices with their start and end apart: 7, of which 2 were waited for; matrix products, arithmetic and copies ran while one was open for 0% of the time, Pallas kernels for 3%

profile of v2, /device:TPU:1, one launch (start us, length us, event | category | flops | bytes accessed | tf_op | source)
XLA Modules:
  0.0 104.7 jit_solution(12508104555992116841)
XLA Ops:
  0.6 1.7 %shard_map.143 = f32[32,1,128]{2,1,0:T(1,128)} custom-call(bf16[1,4,16384]{2,1,0:T(4,128)(2,1)} %refs_2_.3, bf16[1,4,2048]{2,1,0:T(4,128)(2,1)} %refs_6_.3), custom_call_target="tpu_custom_call" | custom-call | tf_op jit(solution)/shard_map/pallas_call | solution.py:108
  2.3 28.5 %all_to_all.15.got_ref = f32[32,1,128]{2,1,0:T(1,128)S(1)} all-to-all(f32[32,1,128]{2,1,0:T(1,128)} %shard_map.143), channel_id=1, replica_groups=mesh['zl'=4,'core'=2,'zh'=4,'y'=4,'x'=4] {'zh','zl','core'}, dimensions={0} | all-to-all | bytes 32768 | tf_op jit(solution)/shard_map/all_to_all | solution.py:95
  30.8 13.1 %all_to_all.16.refs_0_ = f32[16,1,128]{2,1,0:T(1,128)} all-to-all(f32[16,1,128]{2,1,0:T(1,128)S(1)} %shard_map.144), channel_id=1, replica_groups=mesh['zl'=4,'core'=2,'zh'=4,'y'=4,'x'=4] {'y','x'}, dimensions={0} | all-to-all | bytes 16384 | tf_op jit(solution)/shard_map/all_to_all | solution.py:95
  43.9 2.4 %shard_map.145 = (bf16[64,2,4,256]{3,2,1,0:T(4,128)(2,1)}, f32[1,1]{1,0:T(1,128)}) custom-call(f32[16,1,128]{2,1,0:T(1,128)} %all_to_all.16.refs_0_, f32[1,4,16384]{2,1,0:T(4,128)} %refs_1_.3, bf16[1,4,16384]{2,1,0:T(4,128)(2,1)} %refs_2_.3, f32[1,4,16384]{2,1,0:T(4,128)} %refs_3_.3, f32[1,4,16384]{2,1,0:T(4,128)} %refs_4_.3, f32[1,4,2048]{2,1,0:T(4,128)} %refs_5_.3, ...), custom_call_target="tpu_custom_call" | custom-call | tf_op jit(solution)/shard_map/pallas_call | solution.py:117
  46.2 23.1 %all_to_all.17 = bf16[64,2,4,256]{3,2,1,0:T(4,128)(2,1)S(1)} all-to-all(bf16[64,2,4,256]{3,2,1,0:T(4,128)(2,1)} %get-tuple-element.27), channel_id=1, replica_groups=mesh['zl'=4,'core'=2,'zh'=4,'y'=4,'x'=4] {'zh','y','x'}, dimensions={0} | all-to-all | bytes 524288 | tf_op jit(solution)/shard_map/all_to_all | solution.py:95
  69.3 0.1 copy.16
  69.4 0.1 reshape.19.refs_0_
  69.5 6.6 %collective-permute-start.2 = (bf16[2,256,256]{2,1,0:T(8,128)(2,1)S(1)}, bf16[2,256,256]{2,1,0:T(8,128)(2,1)S(1)}, u32[]{:S(2)}, u32[]{:S(2)}) collective-permute-start(bf16[2,256,256]{2,1,0:T(8,128)(2,1)S(1)} %reshape.19.refs_0_), channel_id=1, source_target_pairs={{0,384},{128,256},{256,128},{384,0},{1,385},{129,257},{257,129},{3... | collective-permute-start | bytes 786440 | tf_op jit(solution)/shard_map/ppermute | solution.py:146
  76.1 3.2 %collective-permute-start.1 = (bf16[2,256,256]{2,1,0:T(8,128)(2,1)S(1)}, bf16[2,256,256]{2,1,0:T(8,128)(2,1)S(1)}, u32[]{:S(2)}, u32[]{:S(2)}) collective-permute-start(bf16[2,256,256]{2,1,0:T(8,128)(2,1)S(1)} %reshape.19.refs_0_), channel_id=1, source_target_pairs={{0,128},{128,0},{256,384},{384,256},{1,129},{129,1},{257,385},{385... | collective-permute-start | bytes 786440 | tf_op jit(solution)/shard_map/ppermute | solution.py:146
  79.4 1.9 %collective-permute-start = (bf16[2,256,256]{2,1,0:T(8,128)(2,1)S(1)}, bf16[2,256,256]{2,1,0:T(8,128)(2,1)S(1)}, u32[]{:S(2)}, u32[]{:S(2)}) collective-permute-start(bf16[2,256,256]{2,1,0:T(8,128)(2,1)S(1)} %reshape.19.refs_0_), channel_id=1, source_target_pairs={{0,256},{128,384},{256,0},{384,128},{1,257},{129,385},{257,1},{385... | collective-permute-start | bytes 786440 | tf_op jit(solution)/shard_map/ppermute | solution.py:146
  81.3 3.0 %shard_map.146 = (f32[1,4,16384]{2,1,0:T(4,128)}, f32[1,4,16384]{2,1,0:T(4,128)}, f32[1,4,16384]{2,1,0:T(4,128)}, f32[1,4,2048]{2,1,0:T(4,128)}, f32[1,4,2048]{2,1,0:T(4,128)}, /*index=5*/f32[1,4,2048]{2,1,0:T(4,128)}) custom-call(f32[1,1]{1,0:T(1,128)} %get-tuple-element.30.refs_0_, f32[1,4,16384]{2,1,0:T(4,128)} %refs_1_.3, bf16[1,4,16384]{2,1,0:T(4,128)(2,1)} %refs_2_.3, ...), custom_call_target="tpu_custom_call" | custom-call | flops 1474560 | bytes 1916928 | tf_op jit(solution)/shard_map/pallas_call | solution.py:130
  84.2 6.3 %collective-permute-start.3 = (bf16[2,256,256]{2,1,0:T(8,128)(2,1)S(1)}, bf16[2,256,256]{2,1,0:T(8,128)(2,1)S(1)}, u32[]{:S(2)}, u32[]{:S(2)}) collective-permute-start(bf16[2,256,256]{2,1,0:T(8,128)(2,1)S(1)} %reshape.19.refs_0_), channel_id=1, source_target_pairs={{0,64},{64,0},{1,65},{65,1},{2,66},{66,2},{3,67},{67,3},{4,68},{68... | collective-permute-start | bytes 786440 | tf_op jit(solution)/shard_map/ppermute | solution.py:148
  90.5 0.0 collective-permute-done.2.refs_3_
  90.5 1.9 %collective-permute-start.6 = (bf16[2,256,256]{2,1,0:T(8,128)(2,1)S(1)}, bf16[2,256,256]{2,1,0:T(8,128)(2,1)S(1)}, u32[]{:S(2)}, u32[]{:S(2)}) collective-permute-start(bf16[2,256,256]{2,1,0:T(8,128)(2,1)S(1)} %collective-permute-done.2.refs_3_), channel_id=1, source_target_pairs={{0,64},{64,0},{1,65},{65,1},{2,66},{66,2},{3,67},{67,3},{4,68},{68... | collective-permute-start | bytes 786440 | tf_op jit(solution)/shard_map/ppermute | solution.py:148
  92.4 0.0 collective-permute-done.1.refs_2_
  92.5 2.4 %collective-permute-start.5 = (bf16[2,256,256]{2,1,0:T(8,128)(2,1)S(1)}, bf16[2,256,256]{2,1,0:T(8,128)(2,1)S(1)}, u32[]{:S(2)}, u32[]{:S(2)}) collective-permute-start(bf16[2,256,256]{2,1,0:T(8,128)(2,1)S(1)} %collective-permute-done.1.refs_2_), channel_id=1, source_target_pairs={{0,64},{64,0},{1,65},{65,1},{2,66},{66,2},{3,67},{67,3},{4,68},{68... | collective-permute-start | bytes 786440 | tf_op jit(solution)/shard_map/ppermute | solution.py:148
  94.9 2.7 %collective-permute-done.refs_1_ = bf16[2,256,256]{2,1,0:T(8,128)(2,1)S(1)} collective-permute-done((bf16[2,256,256]{2,1,0:T(8,128)(2,1)S(1)}, bf16[2,256,256]{2,1,0:T(8,128)(2,1)S(1)}, u32[]{:S(2)}, u32[]{:S(2)}) %collective-permute-start) | collective-permute-done | bytes 262176 | tf_op jit(solution)/shard_map/ppermute | solution.py:146
  97.6 4.5 %collective-permute-start.4 = (bf16[2,256,256]{2,1,0:T(8,128)(2,1)S(1)}, bf16[2,256,256]{2,1,0:T(8,128)(2,1)S(1)}, u32[]{:S(2)}, u32[]{:S(2)}) collective-permute-start(bf16[2,256,256]{2,1,0:T(8,128)(2,1)S(1)} %collective-permute-done.refs_1_), channel_id=1, source_target_pairs={{0,64},{64,0},{1,65},{65,1},{2,66},{66,2},{3,67},{67,3},{4,68},{68... | collective-permute-start | bytes 786440 | tf_op jit(solution)/shard_map/ppermute | solution.py:148
  102.1 0.0 collective-permute-done.3.refs_4_
  102.1 0.0 collective-permute-done.6.refs_7_
  102.1 0.0 collective-permute-done.5.refs_6_
  102.1 1.1 %collective-permute-done.4.refs_5_ = bf16[2,256,256]{2,1,0:T(8,128)(2,1)S(1)} collective-permute-done((bf16[2,256,256]{2,1,0:T(8,128)(2,1)S(1)}, bf16[2,256,256]{2,1,0:T(8,128)(2,1)S(1)}, u32[]{:S(2)}, u32[]{:S(2)}) %collective-permute-start.4) | collective-permute-done | bytes 262176 | tf_op jit(solution)/shard_map/ppermute | solution.py:148
  103.2 1.4 %shard_map.147 = (bf16[8,256,256]{2,1,0:T(8,128)(2,1)}, bf16[8,256,256]{2,1,0:T(8,128)(2,1)}) custom-call(bf16[2,256,256]{2,1,0:T(8,128)(2,1)S(1)} %reshape.19.refs_0_, bf16[2,256,256]{2,1,0:T(8,128)(2,1)S(1)} %collective-permute-done.refs_1_, bf16[2,256,256]{2,1,0:T(8,128)(2,1)S(1)} %collective-permute-done.1.refs_2_, ...), custom_call_target="tpu_custom_call" | custom-call | tf_op jit(solution)/shard_map/pallas_call | solution.py:150
  (1 shorter events, 0.0 us)
Async XLA Ops:
  69.5 21.0 %collective-permute-start.2 = (bf16[2,256,256]{2,1,0:T(8,128)(2,1)S(1)}, bf16[2,256,256]{2,1,0:T(8,128)(2,1)S(1)}, u32[]{:S(2)}, u32[]{:S(2)}) collective-permute-start(bf16[2,256,256]{2,1,0:T(8,128)(2,1)S(1)} %reshape.19.refs_0_), channel_id=1, source_target_pairs={{0,384},{128,256},{256,128},{384,0},{1,385},{129,257},{257,129},{3... | collective-permute-start | bytes 786440 | tf_op jit(solution)/shard_map/ppermute | solution.py:146
  76.1 16.4 %collective-permute-start.1 = (bf16[2,256,256]{2,1,0:T(8,128)(2,1)S(1)}, bf16[2,256,256]{2,1,0:T(8,128)(2,1)S(1)}, u32[]{:S(2)}, u32[]{:S(2)}) collective-permute-start(bf16[2,256,256]{2,1,0:T(8,128)(2,1)S(1)} %reshape.19.refs_0_), channel_id=1, source_target_pairs={{0,128},{128,0},{256,384},{384,256},{1,129},{129,1},{257,385},{385... | collective-permute-start | bytes 786440 | tf_op jit(solution)/shard_map/ppermute | solution.py:146
  79.4 18.2 %collective-permute-start = (bf16[2,256,256]{2,1,0:T(8,128)(2,1)S(1)}, bf16[2,256,256]{2,1,0:T(8,128)(2,1)S(1)}, u32[]{:S(2)}, u32[]{:S(2)}) collective-permute-start(bf16[2,256,256]{2,1,0:T(8,128)(2,1)S(1)} %reshape.19.refs_0_), channel_id=1, source_target_pairs={{0,256},{128,384},{256,0},{384,128},{1,257},{129,385},{257,1},{385... | collective-permute-start | bytes 786440 | tf_op jit(solution)/shard_map/ppermute | solution.py:146
  84.2 17.9 %collective-permute-start.3 = (bf16[2,256,256]{2,1,0:T(8,128)(2,1)S(1)}, bf16[2,256,256]{2,1,0:T(8,128)(2,1)S(1)}, u32[]{:S(2)}, u32[]{:S(2)}) collective-permute-start(bf16[2,256,256]{2,1,0:T(8,128)(2,1)S(1)} %reshape.19.refs_0_), channel_id=1, source_target_pairs={{0,64},{64,0},{1,65},{65,1},{2,66},{66,2},{3,67},{67,3},{4,68},{68... | collective-permute-start | bytes 786440 | tf_op jit(solution)/shard_map/ppermute | solution.py:148
  90.5 11.6 %collective-permute-start.6 = (bf16[2,256,256]{2,1,0:T(8,128)(2,1)S(1)}, bf16[2,256,256]{2,1,0:T(8,128)(2,1)S(1)}, u32[]{:S(2)}, u32[]{:S(2)}) collective-permute-start(bf16[2,256,256]{2,1,0:T(8,128)(2,1)S(1)} %collective-permute-done.2.refs_3_), channel_id=1, source_target_pairs={{0,64},{64,0},{1,65},{65,1},{2,66},{66,2},{3,67},{67,3},{4,68},{68... | collective-permute-start | bytes 786440 | tf_op jit(solution)/shard_map/ppermute | solution.py:148
  92.5 9.7 %collective-permute-start.5 = (bf16[2,256,256]{2,1,0:T(8,128)(2,1)S(1)}, bf16[2,256,256]{2,1,0:T(8,128)(2,1)S(1)}, u32[]{:S(2)}, u32[]{:S(2)}) collective-permute-start(bf16[2,256,256]{2,1,0:T(8,128)(2,1)S(1)} %collective-permute-done.1.refs_2_), channel_id=1, source_target_pairs={{0,64},{64,0},{1,65},{65,1},{2,66},{66,2},{3,67},{67,3},{4,68},{68... | collective-permute-start | bytes 786440 | tf_op jit(solution)/shard_map/ppermute | solution.py:148
  97.6 5.7 %collective-permute-start.4 = (bf16[2,256,256]{2,1,0:T(8,128)(2,1)S(1)}, bf16[2,256,256]{2,1,0:T(8,128)(2,1)S(1)}, u32[]{:S(2)}, u32[]{:S(2)}) collective-permute-start(bf16[2,256,256]{2,1,0:T(8,128)(2,1)S(1)} %collective-permute-done.refs_1_), channel_id=1, source_target_pairs={{0,64},{64,0},{1,65},{65,1},{2,66},{66,2},{3,67},{67,3},{4,68},{68... | collective-permute-start | bytes 786440 | tf_op jit(solution)/shard_map/ppermute | solution.py:148

commit v3 on v2

--- a/solution.py
+++ b/solution.py
@@ -9,6 +9,7 @@
 KV_HEADS = 8
 HD = 128
 LANES = 128
+GRADS = (1, 5)
 GROUP = ("zl", "core")
 SHARD = ("zh", "y", "x")
 RING = ("zh", "zl", "core")
@@ -16,7 +17,7 @@
 TURNS = (0, 2, 1, 3)
 VMEM = pl.BlockSpec(memory_space=pltpu.VMEM)
 ANY = pl.BlockSpec(memory_space=pl.ANY)
-WIDE = pltpu.CompilerParams(vmem_limit_bytes=60 * 1024 * 1024)
+HBM = pl.BlockSpec(memory_space=pltpu.HBM)
 SLIM = pltpu.CompilerParams(vmem_limit_bytes=8 * 1024 * 1024)
 
 
@@ -31,14 +32,23 @@
     return (param_new, first_new, second_new)
 
 
-def squares_kernel(out_ref, pair_ref, sums_ref):
+def load_kernel(*refs):
+    given, held, sums_ref, sems = refs[:8], refs[8:16], refs[16], refs[17]
+    order = GRADS + tuple(i for i in range(8) if i not in GRADS)
+    copies = {i: pltpu.make_async_copy(given[i], held[i], sems.at[i]) for i in order}
+    for i in order:
+        copies[i].start()
     total = jnp.zeros((4, LANES), jnp.float32)
-    for ref in (pair_ref, out_ref):
-        for at in range(0, ref.shape[2], LANES):
-            wide = ref[0, :, at : at + LANES].astype(jnp.float32)
+    for i in GRADS:
+        copies[i].wait()
+    for i in GRADS:
+        for at in range(0, held[i].shape[2], LANES):
+            wide = held[i][0, :, at : at + LANES].astype(jnp.float32)
             total = total + wide * wide
     row = jnp.sum(total, axis=0, keepdims=True)
     sums_ref[...] = jnp.broadcast_to(row[None], sums_ref.shape)
+    for i in order[2:]:
+        copies[i].wait()
 
 
 def add_kernel(got_ref, sums_ref):
@@ -105,10 +115,14 @@
     def sums(axes):
         return jax.ShapeDtypeStruct((lax.axis_size(axes), 1, LANES), jnp.float32)
 
-    squares = pl.pallas_call(
-        squares_kernel, out_shape=sums(RING), in_specs=[VMEM] * 2, out_specs=VMEM,
-        compiler_params=WIDE,
-    )(given[1], given[5])
+    *held, squares = pl.pallas_call(
+        load_kernel,
+        out_shape=[jax.ShapeDtypeStruct(x.shape, x.dtype) for x in given] + [sums(RING)],
+        in_specs=[HBM] * 8,
+        out_specs=[VMEM] * 9,
+        scratch_shapes=[pltpu.SemaphoreType.DMA((8,))],
+        compiler_params=SLIM,
+    )(*[pltpu.with_memory_space_constraint(x, pltpu.HBM) for x in given])
     ring_sums = pl.pallas_call(
         add_kernel, out_shape=sums(PLANE), in_specs=[VMEM], out_specs=VMEM,
         compiler_params=SLIM,
@@ -122,8 +136,8 @@
         ),
         in_specs=[VMEM] * 9,
         out_specs=(VMEM, VMEM),
-        compiler_params=WIDE,
-    )(plane_sums, *given)
+        compiler_params=SLIM,
+    )(plane_sums, *held)
     mine = swap(sent, SHARD)
 
     mine, factor = lax.optimization_barrier((mine, factor))
@@ -134,11 +148,11 @@
         ],
         in_specs=[VMEM] * 9,
         out_specs=[VMEM] * 6,
-        compiler_params=WIDE,
+        compiler_params=SLIM,
         cost_estimate=pl.CostEstimate(
             flops=20 * count // devices, bytes_accessed=26 * count // devices, transcendentals=0
         ),
-    )(factor, *given)
+    )(factor, *held)
 
     mine = jnp.transpose(mine, (1, 0, 2, 3)).reshape(2, shards * rows, width)
     near = [mine]

time: 105 us -> 103 us (0.981)
  Pallas kernels: 8.47 us -> 5.16 us
  waiting for transfers between devices: 3.84 us -> 5.24 us
    pallas_call x1, Pallas kernels: 2.36 us -> 0.66 us  [per_device(): pl.pallas_call(lambda *refs: send_kernel(count, *refs), out_shape=(jax.Sh...]
    ppermute x3, waiting for transfers between devices: 2.73 us -> 4.12 us  [per_device(): near.append(lax.ppermute(mine, 'zl', [(i, i ^ k) for i in range(4)]))]
    pallas_call x1, Pallas kernels: 2.96 us -> 1.75 us  [per_device(): pl.pallas_call(state_kernel, out_shape=[jax.ShapeDtypeStruct(given[i].sha...]
  transfers between devices with their start and end apart: 7 -> 7, of which waited for: 2 -> 2; matrix products, arithmetic and copies ran while one was open for 0% -> 0% of each run, Pallas kernels for 3% -> 2%
where the time goes in v3:
time: 103 us; the launch traced here: 102 us
  blocking collectives  63.8 us (62%)
  starting transfers between devices  27.1 us (26%)
  waiting for transfers between devices  5.24 us (5%)
  Pallas kernels  5.16 us (5%)
    all_to_all x3, blocking collectives, swap(): return lax.all_to_all(value, axes, split_axis=0, concat_axis=0, tiled=True)  63.8 us
    ppermute x4, starting transfers between devices, per_device(): far = [lax.ppermute(block, 'core', [(0, 1), (1, 0)]) for block in near]  14.9 us
    ppermute x3, starting transfers between devices, per_device(): near.append(lax.ppermute(mine, 'zl', [(i, i ^ k) for i in range(4)]))  12.2 us
    ppermute x3, waiting for transfers between devices, per_device(): near.append(lax.ppermute(mine, 'zl', [(i, i ^ k) for i in range(4)]))  4.12 us
  transfers between devices with their start and end apart: 7, of which 2 were waited for; matrix products, arithmetic and copies ran while one was open for 0% of the time, Pallas kernels for 2%

profile of v3, /device:TPU:1, one launch (start us, length us, event | category | flops | bytes accessed | tf_op | source)
XLA Modules:
  0.0 102.2 jit_solution(8627213138856793515)
XLA Ops:
  0.6 1.3 %shard_map.143 = (f32[1,4,16384]{2,1,0:T(4,128)S(1)}, bf16[1,4,16384]{2,1,0:T(4,128)(2,1)S(1)}, f32[1,4,16384]{2,1,0:T(4,128)S(1)}, f32[1,4,16384]{2,1,0:T(4,128...) custom-call(f32[1,4,16384]{2,1,0:T(4,128)} %refs_0_.1, ...), custom_call_target="tpu_custom_call" | custom-call | tf_op jit(solution)/shard_map/pallas_call | solution.py:118
  1.9 28.3 %all_to_all.15.got_ref = f32[32,1,128]{2,1,0:T(1,128)S(1)} all-to-all(f32[32,1,128]{2,1,0:T(1,128)S(1)} %get-tuple-element.36), channel_id=1, replica_groups=mesh['zl'=4,'core'=2,'zh'=4,'y'=4,'x'=4] {'zh','zl','core'}, dimensions={0} | all-to-all | bytes 32768 | tf_op jit(solution)/shard_map/all_to_all | solution.py:105
  30.3 13.0 %all_to_all.16.refs_0_ = f32[16,1,128]{2,1,0:T(1,128)S(1)} all-to-all(f32[16,1,128]{2,1,0:T(1,128)S(1)} %shard_map.144), channel_id=1, replica_groups=mesh['zl'=4,'core'=2,'zh'=4,'y'=4,'x'=4] {'y','x'}, dimensions={0} | all-to-all | bytes 16384 | tf_op jit(solution)/shard_map/all_to_all | solution.py:105
  43.3 0.7 shard_map.145
  43.9 22.5 %all_to_all.17 = bf16[64,2,4,256]{3,2,1,0:T(4,128)(2,1)S(1)} all-to-all(bf16[64,2,4,256]{3,2,1,0:T(4,128)(2,1)S(1)} %get-tuple-element.45), channel_id=1, replica_groups=mesh['zl'=4,'core'=2,'zh'=4,'y'=4,'x'=4] {'zh','y','x'}, dimensions={0} | all-to-all | bytes 524288 | tf_op jit(solution)/shard_map/all_to_all | solution.py:105
  66.4 0.1 copy.16
  66.5 0.1 reshape.19.refs_0_
  66.6 7.0 %collective-permute-start.2 = (bf16[2,256,256]{2,1,0:T(8,128)(2,1)S(1)}, bf16[2,256,256]{2,1,0:T(8,128)(2,1)S(1)}, u32[]{:S(2)}, u32[]{:S(2)}) collective-permute-start(bf16[2,256,256]{2,1,0:T(8,128)(2,1)S(1)} %reshape.19.refs_0_), channel_id=1, source_target_pairs={{0,384},{128,256},{256,128},{384,0},{1,385},{129,257},{257,129},{3... | collective-permute-start | bytes 786440 | tf_op jit(solution)/shard_map/ppermute | solution.py:160
  73.6 3.2 %collective-permute-start.1 = (bf16[2,256,256]{2,1,0:T(8,128)(2,1)S(1)}, bf16[2,256,256]{2,1,0:T(8,128)(2,1)S(1)}, u32[]{:S(2)}, u32[]{:S(2)}) collective-permute-start(bf16[2,256,256]{2,1,0:T(8,128)(2,1)S(1)} %reshape.19.refs_0_), channel_id=1, source_target_pairs={{0,128},{128,0},{256,384},{384,256},{1,129},{129,1},{257,385},{385... | collective-permute-start | bytes 786440 | tf_op jit(solution)/shard_map/ppermute | solution.py:160
  76.8 1.9 %collective-permute-start = (bf16[2,256,256]{2,1,0:T(8,128)(2,1)S(1)}, bf16[2,256,256]{2,1,0:T(8,128)(2,1)S(1)}, u32[]{:S(2)}, u32[]{:S(2)}) collective-permute-start(bf16[2,256,256]{2,1,0:T(8,128)(2,1)S(1)} %reshape.19.refs_0_), channel_id=1, source_target_pairs={{0,256},{128,384},{256,0},{384,128},{1,257},{129,385},{257,1},{385... | collective-permute-start | bytes 786440 | tf_op jit(solution)/shard_map/ppermute | solution.py:160
  78.8 1.8 %shard_map.146 = (f32[1,4,16384]{2,1,0:T(4,128)}, f32[1,4,16384]{2,1,0:T(4,128)}, f32[1,4,16384]{2,1,0:T(4,128)}, f32[1,4,2048]{2,1,0:T(4,128)}, f32[1,4,2048]{2,1,0:T(4,128)}, /*index=5*/f32[1,4,2048]{2,1,0:T(4,128)}) custom-call(f32[1,1]{1,0:T(1,128)} %get-tuple-element.48.refs_0_, f32[1,4,16384]{2,1,0:T(4,128)S(1)} %get-tuple-element.37.refs_1_, ...), custom_call_target="tpu_custom_call" | custom-call | flops 1474560 | bytes 1916928 | tf_op jit(solution)/shard_map/pallas_call | solution.py:144
  80.5 6.3 %collective-permute-start.3 = (bf16[2,256,256]{2,1,0:T(8,128)(2,1)S(1)}, bf16[2,256,256]{2,1,0:T(8,128)(2,1)S(1)}, u32[]{:S(2)}, u32[]{:S(2)}) collective-permute-start(bf16[2,256,256]{2,1,0:T(8,128)(2,1)S(1)} %reshape.19.refs_0_), channel_id=1, source_target_pairs={{0,64},{64,0},{1,65},{65,1},{2,66},{66,2},{3,67},{67,3},{4,68},{68... | collective-permute-start | bytes 786440 | tf_op jit(solution)/shard_map/ppermute | solution.py:162
  86.8 0.0 collective-permute-done.2.refs_3_
  86.8 1.9 %collective-permute-start.6 = (bf16[2,256,256]{2,1,0:T(8,128)(2,1)S(1)}, bf16[2,256,256]{2,1,0:T(8,128)(2,1)S(1)}, u32[]{:S(2)}, u32[]{:S(2)}) collective-permute-start(bf16[2,256,256]{2,1,0:T(8,128)(2,1)S(1)} %collective-permute-done.2.refs_3_), channel_id=1, source_target_pairs={{0,64},{64,0},{1,65},{65,1},{2,66},{66,2},{3,67},{67,3},{4,68},{68... | collective-permute-start | bytes 786440 | tf_op jit(solution)/shard_map/ppermute | solution.py:162
  88.7 0.0 collective-permute-done.1.refs_2_
  88.7 2.4 %collective-permute-start.5 = (bf16[2,256,256]{2,1,0:T(8,128)(2,1)S(1)}, bf16[2,256,256]{2,1,0:T(8,128)(2,1)S(1)}, u32[]{:S(2)}, u32[]{:S(2)}) collective-permute-start(bf16[2,256,256]{2,1,0:T(8,128)(2,1)S(1)} %collective-permute-done.1.refs_2_), channel_id=1, source_target_pairs={{0,64},{64,0},{1,65},{65,1},{2,66},{66,2},{3,67},{67,3},{4,68},{68... | collective-permute-start | bytes 786440 | tf_op jit(solution)/shard_map/ppermute | solution.py:162
  91.2 4.1 %collective-permute-done.refs_1_ = bf16[2,256,256]{2,1,0:T(8,128)(2,1)S(1)} collective-permute-done((bf16[2,256,256]{2,1,0:T(8,128)(2,1)S(1)}, bf16[2,256,256]{2,1,0:T(8,128)(2,1)S(1)}, u32[]{:S(2)}, u32[]{:S(2)}) %collective-permute-start) | collective-permute-done | bytes 262176 | tf_op jit(solution)/shard_map/ppermute | solution.py:160
  95.3 4.3 %collective-permute-start.4 = (bf16[2,256,256]{2,1,0:T(8,128)(2,1)S(1)}, bf16[2,256,256]{2,1,0:T(8,128)(2,1)S(1)}, u32[]{:S(2)}, u32[]{:S(2)}) collective-permute-start(bf16[2,256,256]{2,1,0:T(8,128)(2,1)S(1)} %collective-permute-done.refs_1_), channel_id=1, source_target_pairs={{0,64},{64,0},{1,65},{65,1},{2,66},{66,2},{3,67},{67,3},{4,68},{68... | collective-permute-start | bytes 786440 | tf_op jit(solution)/shard_map/ppermute | solution.py:162
  99.6 0.0 collective-permute-done.3.refs_4_
  99.6 0.0 collective-permute-done.6.refs_7_
  99.6 0.0 collective-permute-done.5.refs_6_
  99.6 1.1 %collective-permute-done.4.refs_5_ = bf16[2,256,256]{2,1,0:T(8,128)(2,1)S(1)} collective-permute-done((bf16[2,256,256]{2,1,0:T(8,128)(2,1)S(1)}, bf16[2,256,256]{2,1,0:T(8,128)(2,1)S(1)}, u32[]{:S(2)}, u32[]{:S(2)}) %collective-permute-start.4) | collective-permute-done | bytes 262176 | tf_op jit(solution)/shard_map/ppermute | solution.py:162
  100.7 1.4 %shard_map.147 = (bf16[8,256,256]{2,1,0:T(8,128)(2,1)}, bf16[8,256,256]{2,1,0:T(8,128)(2,1)}) custom-call(bf16[2,256,256]{2,1,0:T(8,128)(2,1)S(1)} %reshape.19.refs_0_, bf16[2,256,256]{2,1,0:T(8,128)(2,1)S(1)} %collective-permute-done.refs_1_, bf16[2,256,256]{2,1,0:T(8,128)(2,1)S(1)} %collective-permute-done.1.refs_2_, ...), custom_call_target="tpu_custom_call" | custom-call | tf_op jit(solution)/shard_map/pallas_call | solution.py:164
  (1 shorter events, 0.0 us)
Async XLA Ops:
  66.6 20.2 %collective-permute-start.2 = (bf16[2,256,256]{2,1,0:T(8,128)(2,1)S(1)}, bf16[2,256,256]{2,1,0:T(8,128)(2,1)S(1)}, u32[]{:S(2)}, u32[]{:S(2)}) collective-permute-start(bf16[2,256,256]{2,1,0:T(8,128)(2,1)S(1)} %reshape.19.refs_0_), channel_id=1, source_target_pairs={{0,384},{128,256},{256,128},{384,0},{1,385},{129,257},{257,129},{3... | collective-permute-start | bytes 786440 | tf_op jit(solution)/shard_map/ppermute | solution.py:160
  73.6 15.2 %collective-permute-start.1 = (bf16[2,256,256]{2,1,0:T(8,128)(2,1)S(1)}, bf16[2,256,256]{2,1,0:T(8,128)(2,1)S(1)}, u32[]{:S(2)}, u32[]{:S(2)}) collective-permute-start(bf16[2,256,256]{2,1,0:T(8,128)(2,1)S(1)} %reshape.19.refs_0_), channel_id=1, source_target_pairs={{0,128},{128,0},{256,384},{384,256},{1,129},{129,1},{257,385},{385... | collective-permute-start | bytes 786440 | tf_op jit(solution)/shard_map/ppermute | solution.py:160
  76.8 18.4 %collective-permute-start = (bf16[2,256,256]{2,1,0:T(8,128)(2,1)S(1)}, bf16[2,256,256]{2,1,0:T(8,128)(2,1)S(1)}, u32[]{:S(2)}, u32[]{:S(2)}) collective-permute-start(bf16[2,256,256]{2,1,0:T(8,128)(2,1)S(1)} %reshape.19.refs_0_), channel_id=1, source_target_pairs={{0,256},{128,384},{256,0},{384,128},{1,257},{129,385},{257,1},{385... | collective-permute-start | bytes 786440 | tf_op jit(solution)/shard_map/ppermute | solution.py:160
  80.5 19.1 %collective-permute-start.3 = (bf16[2,256,256]{2,1,0:T(8,128)(2,1)S(1)}, bf16[2,256,256]{2,1,0:T(8,128)(2,1)S(1)}, u32[]{:S(2)}, u32[]{:S(2)}) collective-permute-start(bf16[2,256,256]{2,1,0:T(8,128)(2,1)S(1)} %reshape.19.refs_0_), channel_id=1, source_target_pairs={{0,64},{64,0},{1,65},{65,1},{2,66},{66,2},{3,67},{67,3},{4,68},{68... | collective-permute-start | bytes 786440 | tf_op jit(solution)/shard_map/ppermute | solution.py:162
  86.8 12.8 %collective-permute-start.6 = (bf16[2,256,256]{2,1,0:T(8,128)(2,1)S(1)}, bf16[2,256,256]{2,1,0:T(8,128)(2,1)S(1)}, u32[]{:S(2)}, u32[]{:S(2)}) collective-permute-start(bf16[2,256,256]{2,1,0:T(8,128)(2,1)S(1)} %collective-permute-done.2.refs_3_), channel_id=1, source_target_pairs={{0,64},{64,0},{1,65},{65,1},{2,66},{66,2},{3,67},{67,3},{4,68},{68... | collective-permute-start | bytes 786440 | tf_op jit(solution)/shard_map/ppermute | solution.py:162
  88.7 10.9 %collective-permute-start.5 = (bf16[2,256,256]{2,1,0:T(8,128)(2,1)S(1)}, bf16[2,256,256]{2,1,0:T(8,128)(2,1)S(1)}, u32[]{:S(2)}, u32[]{:S(2)}) collective-permute-start(bf16[2,256,256]{2,1,0:T(8,128)(2,1)S(1)} %collective-permute-done.1.refs_2_), channel_id=1, source_target_pairs={{0,64},{64,0},{1,65},{65,1},{2,66},{66,2},{3,67},{67,3},{4,68},{68... | collective-permute-start | bytes 786440 | tf_op jit(solution)/shard_map/ppermute | solution.py:162
  95.3 5.4 %collective-permute-start.4 = (bf16[2,256,256]{2,1,0:T(8,128)(2,1)S(1)}, bf16[2,256,256]{2,1,0:T(8,128)(2,1)S(1)}, u32[]{:S(2)}, u32[]{:S(2)}) collective-permute-start(bf16[2,256,256]{2,1,0:T(8,128)(2,1)S(1)} %collective-permute-done.refs_1_), channel_id=1, source_target_pairs={{0,64},{64,0},{1,65},{65,1},{2,66},{66,2},{3,67},{67,3},{4,68},{68... | collective-permute-start | bytes 786440 | tf_op jit(solution)/shard_map/ppermute | solution.py:162

commit v4 on v3

--- a/solution.py
+++ b/solution.py
@@ -87,18 +87,33 @@
                 ref[0, :, at : at + size] = value
 
 
-def place_kernel(*refs):
-    blocks, out_ref, pair_ref, sems = refs[:8], refs[8], refs[9], refs[10]
+def place_kernel(turns, *refs):
+    blocks, (out_ref, pair_ref, sems) = refs[: 2 * len(turns)], refs[-3:]
     zl, core = lax.axis_index("zl"), lax.axis_index("core")
     copies = []
     for i, ref in enumerate(blocks):
-        layer = 2 * (zl ^ TURNS[i % 4]) + (core if i < 4 else 1 - core)
+        layer = 2 * (zl ^ turns[i // 2]) + (1 - core if i % 2 else core)
         copies.append(pltpu.make_async_copy(ref.at[0], out_ref.at[layer], sems.at[i, 0]))
         copies.append(pltpu.make_async_copy(ref.at[1], pair_ref.at[layer], sems.at[i, 1]))
     for copy in copies:
         copy.start()
     for copy in copies:
         copy.wait()
+
+
+def place(turns, blocks, shape, begun):
+    return pl.pallas_call(
+        lambda *refs: place_kernel(turns, *refs),
+        out_shape=(shape, shape),
+        in_specs=[ANY] * (len(blocks) + len(begun)),
+        out_specs=(ANY, ANY),
+        scratch_shapes=[pltpu.SemaphoreType.DMA((len(blocks), 2))],
+        input_output_aliases={len(blocks) + i: i for i in range(len(begun))},
+        compiler_params=SLIM,
+        cost_estimate=pl.CostEstimate(
+            flops=0, bytes_accessed=2 * len(blocks) * 2**18, transcendentals=0
+        ),
+    )(*blocks, *begun)
 
 
 def swap(value, axes):
@@ -160,15 +175,11 @@
         near.append(lax.ppermute(mine, "zl", [(i, i ^ k) for i in range(4)]))
     near[0], state = lax.optimization_barrier((near[0], state))
     far = [lax.ppermute(block, "core", [(0, 1), (1, 0)]) for block in near]
-    serving_shape = jax.ShapeDtypeStruct((groups, shards * rows, width), jnp.bfloat16)
-    serving = pl.pallas_call(
-        place_kernel,
-        out_shape=(serving_shape, serving_shape),
-        in_specs=[ANY] * 8,
-        out_specs=(ANY, ANY),
-        scratch_shapes=[pltpu.SemaphoreType.DMA((8, 2))],
-        compiler_params=SLIM,
-    )(*near, *far)
+    shape = jax.ShapeDtypeStruct((groups, shards * rows, width), jnp.bfloat16)
+    pairs = [(near[i], far[i]) for i in range(4)]
+    early = [block for i in (0, 2, 3) for block in pairs[i]]
+    begun = place([TURNS[i] for i in (0, 2, 3)], early, shape, ())
+    serving = place([TURNS[1]], pairs[1], shape, begun)
     return (*state[:3], serving[0], *state[3:], serving[1])
 
 

time: 103 us -> 102 us (level)
  waiting for transfers between devices: 5.24 us -> 4.13 us
    ppermute x4, waiting for transfers between devices: 1.12 us -> 0.01 us  [per_device(): far = [lax.ppermute(block, 'core', [(0, 1), (1, 0)]) for block in near]]
    pallas_call x1 -> x2, Pallas kernels: 1.44 us -> 2.08 us  [place(): pl.pallas_call(lambda *refs: place_kernel(turns, *refs), out_shape=(shape...]
  transfers between devices with their start and end apart: 7 -> 7, of which waited for: 2 -> 1; matrix products, arithmetic and copies ran while one was open for 0% -> 0% of each run, Pallas kernels for 2% -> 3%
where the time goes in v4:
time: 102 us
  blocking collectives  63.8 us (63%)
  starting transfers between devices  27.1 us (27%)
  Pallas kernels  5.81 us (6%)
  waiting for transfers between devices  4.13 us (4%)
    all_to_all x3, blocking collectives, swap(): return lax.all_to_all(value, axes, split_axis=0, concat_axis=0, tiled=True)  63.8 us
    ppermute x4, starting transfers between devices, per_device(): far = [lax.ppermute(block, 'core', [(0, 1), (1, 0)]) for block in near]  14.9 us
    ppermute x3, starting transfers between devices, per_device(): near.append(lax.ppermute(mine, 'zl', [(i, i ^ k) for i in range(4)]))  12.2 us
    ppermute x3, waiting for transfers between devices, per_device(): near.append(lax.ppermute(mine, 'zl', [(i, i ^ k) for i in range(4)]))  4.12 us
    pallas_call x2, Pallas kernels, place(): pl.pallas_call(lambda *refs: place_kernel(turns, *refs), out_shape=(shape...  2.08 us
  transfers between devices with their start and end apart: 7, of which 1 were waited for; matrix products, arithmetic and copies ran while one was open for 0% of the time, Pallas kernels for 3%

profile of v4, /device:TPU:1, one launch (start us, length us, event | category | flops | bytes accessed | tf_op | source)
XLA Modules:
  0.0 101.7 jit_solution(1068738441331865358)
XLA Ops:
  0.6 1.3 %shard_map.143 = (f32[1,4,16384]{2,1,0:T(4,128)S(1)}, bf16[1,4,16384]{2,1,0:T(4,128)(2,1)S(1)}, f32[1,4,16384]{2,1,0:T(4,128)S(1)}, f32[1,4,16384]{2,1,0:T(4,128...) custom-call(f32[1,4,16384]{2,1,0:T(4,128)} %refs_0_.1, ...), custom_call_target="tpu_custom_call" | custom-call | tf_op jit(solution)/shard_map/pallas_call | solution.py:133
  1.9 28.3 %all_to_all.15.got_ref = f32[32,1,128]{2,1,0:T(1,128)S(1)} all-to-all(f32[32,1,128]{2,1,0:T(1,128)S(1)} %get-tuple-element.38), channel_id=1, replica_groups=mesh['zl'=4,'core'=2,'zh'=4,'y'=4,'x'=4] {'zh','zl','core'}, dimensions={0} | all-to-all | bytes 32768 | tf_op jit(solution)/shard_map/all_to_all | solution.py:120
  30.3 13.0 %all_to_all.16.refs_0_ = f32[16,1,128]{2,1,0:T(1,128)S(1)} all-to-all(f32[16,1,128]{2,1,0:T(1,128)S(1)} %shard_map.144), channel_id=1, replica_groups=mesh['zl'=4,'core'=2,'zh'=4,'y'=4,'x'=4] {'y','x'}, dimensions={0} | all-to-all | bytes 16384 | tf_op jit(solution)/shard_map/all_to_all | solution.py:120
  43.3 0.7 shard_map.145
  43.9 22.5 %all_to_all.17 = bf16[64,2,4,256]{3,2,1,0:T(4,128)(2,1)S(1)} all-to-all(bf16[64,2,4,256]{3,2,1,0:T(4,128)(2,1)S(1)} %get-tuple-element.47), channel_id=1, replica_groups=mesh['zl'=4,'core'=2,'zh'=4,'y'=4,'x'=4] {'zh','y','x'}, dimensions={0} | all-to-all | bytes 524288 | tf_op jit(solution)/shard_map/all_to_all | solution.py:120
  66.4 0.1 copy.18
  66.5 0.1 reshape.19.refs_0_
  66.6 7.0 %collective-permute-start.5 = (bf16[2,256,256]{2,1,0:T(8,128)(2,1)S(1)}, bf16[2,256,256]{2,1,0:T(8,128)(2,1)S(1)}, u32[]{:S(2)}, u32[]{:S(2)}) collective-permute-start(bf16[2,256,256]{2,1,0:T(8,128)(2,1)S(1)} %reshape.19.refs_0_), channel_id=1, source_target_pairs={{0,384},{128,256},{256,128},{384,0},{1,385},{129,257},{257,129},{3... | collective-permute-start | bytes 786440 | tf_op jit(solution)/shard_map/ppermute | solution.py:175
  73.6 3.2 %collective-permute-start.3 = (bf16[2,256,256]{2,1,0:T(8,128)(2,1)S(1)}, bf16[2,256,256]{2,1,0:T(8,128)(2,1)S(1)}, u32[]{:S(2)}, u32[]{:S(2)}) collective-permute-start(bf16[2,256,256]{2,1,0:T(8,128)(2,1)S(1)} %reshape.19.refs_0_), channel_id=1, source_target_pairs={{0,128},{128,0},{256,384},{384,256},{1,129},{129,1},{257,385},{385... | collective-permute-start | bytes 786440 | tf_op jit(solution)/shard_map/ppermute | solution.py:175
  76.8 1.9 %collective-permute-start = (bf16[2,256,256]{2,1,0:T(8,128)(2,1)S(1)}, bf16[2,256,256]{2,1,0:T(8,128)(2,1)S(1)}, u32[]{:S(2)}, u32[]{:S(2)}) collective-permute-start(bf16[2,256,256]{2,1,0:T(8,128)(2,1)S(1)} %reshape.19.refs_0_), channel_id=1, source_target_pairs={{0,256},{128,384},{256,0},{384,128},{1,257},{129,385},{257,1},{385... | collective-permute-start | bytes 786440 | tf_op jit(solution)/shard_map/ppermute | solution.py:175
  78.8 1.8 %shard_map.146 = (f32[1,4,16384]{2,1,0:T(4,128)}, f32[1,4,16384]{2,1,0:T(4,128)}, f32[1,4,16384]{2,1,0:T(4,128)}, f32[1,4,2048]{2,1,0:T(4,128)}, f32[1,4,2048]{2,1,0:T(4,128)}, /*index=5*/f32[1,4,2048]{2,1,0:T(4,128)}) custom-call(f32[1,1]{1,0:T(1,128)} %get-tuple-element.50.refs_0_, f32[1,4,16384]{2,1,0:T(4,128)S(1)} %get-tuple-element.39.refs_1_, ...), custom_call_target="tpu_custom_call" | custom-call | flops 1474560 | bytes 1916928 | tf_op jit(solution)/shard_map/pallas_call | solution.py:159
  80.5 6.3 %collective-permute-start.2 = (bf16[2,256,256]{2,1,0:T(8,128)(2,1)S(1)}, bf16[2,256,256]{2,1,0:T(8,128)(2,1)S(1)}, u32[]{:S(2)}, u32[]{:S(2)}) collective-permute-start(bf16[2,256,256]{2,1,0:T(8,128)(2,1)S(1)} %reshape.19.refs_0_), channel_id=1, source_target_pairs={{0,64},{64,0},{1,65},{65,1},{2,66},{66,2},{3,67},{67,3},{4,68},{68... | collective-permute-start | bytes 786440 | tf_op jit(solution)/shard_map/ppermute | solution.py:177
  86.8 0.0 collective-permute-done.5.refs_4_
  86.8 1.9 %collective-permute-start.6 = (bf16[2,256,256]{2,1,0:T(8,128)(2,1)S(1)}, bf16[2,256,256]{2,1,0:T(8,128)(2,1)S(1)}, u32[]{:S(2)}, u32[]{:S(2)}) collective-permute-start(bf16[2,256,256]{2,1,0:T(8,128)(2,1)S(1)} %collective-permute-done.5.refs_4_), channel_id=1, source_target_pairs={{0,64},{64,0},{1,65},{65,1},{2,66},{66,2},{3,67},{67,3},{4,68},{68... | collective-permute-start | bytes 786440 | tf_op jit(solution)/shard_map/ppermute | solution.py:177
  88.7 0.0 collective-permute-done.3.refs_2_
  88.7 2.4 %collective-permute-start.4 = (bf16[2,256,256]{2,1,0:T(8,128)(2,1)S(1)}, bf16[2,256,256]{2,1,0:T(8,128)(2,1)S(1)}, u32[]{:S(2)}, u32[]{:S(2)}) collective-permute-start(bf16[2,256,256]{2,1,0:T(8,128)(2,1)S(1)} %collective-permute-done.3.refs_2_), channel_id=1, source_target_pairs={{0,64},{64,0},{1,65},{65,1},{2,66},{66,2},{3,67},{67,3},{4,68},{68... | collective-permute-start | bytes 786440 | tf_op jit(solution)/shard_map/ppermute | solution.py:177
  91.2 4.1 %collective-permute-done.refs_0_ = bf16[2,256,256]{2,1,0:T(8,128)(2,1)S(1)} collective-permute-done((bf16[2,256,256]{2,1,0:T(8,128)(2,1)S(1)}, bf16[2,256,256]{2,1,0:T(8,128)(2,1)S(1)}, u32[]{:S(2)}, u32[]{:S(2)}) %collective-permute-start) | collective-permute-done | bytes 262176 | tf_op jit(solution)/shard_map/ppermute | solution.py:175
  95.3 4.3 %collective-permute-start.1 = (bf16[2,256,256]{2,1,0:T(8,128)(2,1)S(1)}, bf16[2,256,256]{2,1,0:T(8,128)(2,1)S(1)}, u32[]{:S(2)}, u32[]{:S(2)}) collective-permute-start(bf16[2,256,256]{2,1,0:T(8,128)(2,1)S(1)} %collective-permute-done.refs_0_), channel_id=1, source_target_pairs={{0,64},{64,0},{1,65},{65,1},{2,66},{66,2},{3,67},{67,3},{4,68},{68... | collective-permute-start | bytes 786440 | tf_op jit(solution)/shard_map/ppermute | solution.py:177
  99.6 0.0 collective-permute-done.2.refs_1_
  99.6 0.0 collective-permute-done.6.refs_5_
  99.6 0.0 collective-permute-done.4.refs_3_
  99.6 1.2 %shard_map.147 = (bf16[8,256,256]{2,1,0:T(8,128)(2,1)}, bf16[8,256,256]{2,1,0:T(8,128)(2,1)}) custom-call(bf16[2,256,256]{2,1,0:T(8,128)(2,1)S(1)} %reshape.19.refs_0_, bf16[2,256,256]{2,1,0:T(8,128)(2,1)S(1)} %collective-permute-done.2.refs_1_, bf16[2,256,256]{2,1,0:T(8,128)(2,1)S(1)} %collective-permute-done.3.refs_2_, ...), custom_call_target="tpu_custom_call" | custom-call | bytes 3145728 | tf_op jit(solution)/shard_map/pallas_call | solution.py:105
  100.9 0.0 collective-permute-done.1.refs_1_
  100.9 0.8 shard_map.148
  (1 shorter events, 0.0 us)
Async XLA Ops:
  66.6 20.2 %collective-permute-start.5 = (bf16[2,256,256]{2,1,0:T(8,128)(2,1)S(1)}, bf16[2,256,256]{2,1,0:T(8,128)(2,1)S(1)}, u32[]{:S(2)}, u32[]{:S(2)}) collective-permute-start(bf16[2,256,256]{2,1,0:T(8,128)(2,1)S(1)} %reshape.19.refs_0_), channel_id=1, source_target_pairs={{0,384},{128,256},{256,128},{384,0},{1,385},{129,257},{257,129},{3... | collective-permute-start | bytes 786440 | tf_op jit(solution)/shard_map/ppermute | solution.py:175
  73.6 15.2 %collective-permute-start.3 = (bf16[2,256,256]{2,1,0:T(8,128)(2,1)S(1)}, bf16[2,256,256]{2,1,0:T(8,128)(2,1)S(1)}, u32[]{:S(2)}, u32[]{:S(2)}) collective-permute-start(bf16[2,256,256]{2,1,0:T(8,128)(2,1)S(1)} %reshape.19.refs_0_), channel_id=1, source_target_pairs={{0,128},{128,0},{256,384},{384,256},{1,129},{129,1},{257,385},{385... | collective-permute-start | bytes 786440 | tf_op jit(solution)/shard_map/ppermute | solution.py:175
  76.8 18.4 %collective-permute-start = (bf16[2,256,256]{2,1,0:T(8,128)(2,1)S(1)}, bf16[2,256,256]{2,1,0:T(8,128)(2,1)S(1)}, u32[]{:S(2)}, u32[]{:S(2)}) collective-permute-start(bf16[2,256,256]{2,1,0:T(8,128)(2,1)S(1)} %reshape.19.refs_0_), channel_id=1, source_target_pairs={{0,256},{128,384},{256,0},{384,128},{1,257},{129,385},{257,1},{385... | collective-permute-start | bytes 786440 | tf_op jit(solution)/shard_map/ppermute | solution.py:175
  80.5 19.1 %collective-permute-start.2 = (bf16[2,256,256]{2,1,0:T(8,128)(2,1)S(1)}, bf16[2,256,256]{2,1,0:T(8,128)(2,1)S(1)}, u32[]{:S(2)}, u32[]{:S(2)}) collective-permute-start(bf16[2,256,256]{2,1,0:T(8,128)(2,1)S(1)} %reshape.19.refs_0_), channel_id=1, source_target_pairs={{0,64},{64,0},{1,65},{65,1},{2,66},{66,2},{3,67},{67,3},{4,68},{68... | collective-permute-start | bytes 786440 | tf_op jit(solution)/shard_map/ppermute | solution.py:177
  86.8 12.8 %collective-permute-start.6 = (bf16[2,256,256]{2,1,0:T(8,128)(2,1)S(1)}, bf16[2,256,256]{2,1,0:T(8,128)(2,1)S(1)}, u32[]{:S(2)}, u32[]{:S(2)}) collective-permute-start(bf16[2,256,256]{2,1,0:T(8,128)(2,1)S(1)} %collective-permute-done.5.refs_4_), channel_id=1, source_target_pairs={{0,64},{64,0},{1,65},{65,1},{2,66},{66,2},{3,67},{67,3},{4,68},{68... | collective-permute-start | bytes 786440 | tf_op jit(solution)/shard_map/ppermute | solution.py:177
  88.7 10.9 %collective-permute-start.4 = (bf16[2,256,256]{2,1,0:T(8,128)(2,1)S(1)}, bf16[2,256,256]{2,1,0:T(8,128)(2,1)S(1)}, u32[]{:S(2)}, u32[]{:S(2)}) collective-permute-start(bf16[2,256,256]{2,1,0:T(8,128)(2,1)S(1)} %collective-permute-done.3.refs_2_), channel_id=1, source_target_pairs={{0,64},{64,0},{1,65},{65,1},{2,66},{66,2},{3,67},{67,3},{4,68},{68... | collective-permute-start | bytes 786440 | tf_op jit(solution)/shard_map/ppermute | solution.py:177
  95.3 5.6 %collective-permute-start.1 = (bf16[2,256,256]{2,1,0:T(8,128)(2,1)S(1)}, bf16[2,256,256]{2,1,0:T(8,128)(2,1)S(1)}, u32[]{:S(2)}, u32[]{:S(2)}) collective-permute-start(bf16[2,256,256]{2,1,0:T(8,128)(2,1)S(1)} %collective-permute-done.refs_0_), channel_id=1, source_target_pairs={{0,64},{64,0},{1,65},{65,1},{2,66},{66,2},{3,67},{67,3},{4,68},{68... | collective-permute-start | bytes 786440 | tf_op jit(solution)/shard_map/ppermute | solution.py:177

commit v5 on v4

--- a/solution.py
+++ b/solution.py
@@ -38,13 +38,14 @@
     copies = {i: pltpu.make_async_copy(given[i], held[i], sems.at[i]) for i in order}
     for i in order:
         copies[i].start()
-    total = jnp.zeros((4, LANES), jnp.float32)
-    for i in GRADS:
+    totals = [jnp.zeros((4, LANES), jnp.float32) for _ in range(4)]
+    for i in reversed(GRADS):
         copies[i].wait()
-    for i in GRADS:
         for at in range(0, held[i].shape[2], LANES):
             wide = held[i][0, :, at : at + LANES].astype(jnp.float32)
-            total = total + wide * wide
+            turn = at // LANES % 4
+            totals[turn] = totals[turn] + wide * wide
+    total = (totals[0] + totals[1]) + (totals[2] + totals[3])
     row = jnp.sum(total, axis=0, keepdims=True)
     sums_ref[...] = jnp.broadcast_to(row[None], sums_ref.shape)
     for i in order[2:]:
@@ -95,8 +96,8 @@
         layer = 2 * (zl ^ turns[i // 2]) + (1 - core if i % 2 else core)
         copies.append(pltpu.make_async_copy(ref.at[0], out_ref.at[layer], sems.at[i, 0]))
         copies.append(pltpu.make_async_copy(ref.at[1], pair_ref.at[layer], sems.at[i, 1]))
-    for copy in copies:
-        copy.start()
+    for i, copy in enumerate(copies):
+        copy.start(priority=i % 2)
     for copy in copies:
         copy.wait()
 

time: 102 us -> 102 us (level)
  no operation moved by 1% of the time
where the time goes in v5:
time: 102 us
  blocking collectives  63.8 us (63%)
  starting transfers between devices  27.1 us (27%)
  Pallas kernels  5.81 us (6%)
  waiting for transfers between devices  4.13 us (4%)
    all_to_all x3, blocking collectives, swap(): return lax.all_to_all(value, axes, split_axis=0, concat_axis=0, tiled=True)  63.8 us
    ppermute x4, starting transfers between devices, per_device(): far = [lax.ppermute(block, 'core', [(0, 1), (1, 0)]) for block in near]  14.9 us
    ppermute x3, starting transfers between devices, per_device(): near.append(lax.ppermute(mine, 'zl', [(i, i ^ k) for i in range(4)]))  12.2 us
    ppermute x3, waiting for transfers between devices, per_device(): near.append(lax.ppermute(mine, 'zl', [(i, i ^ k) for i in range(4)]))  4.12 us
    pallas_call x2, Pallas kernels, place(): pl.pallas_call(lambda *refs: place_kernel(turns, *refs), out_shape=(shape...  2.08 us
  transfers between devices with their start and end apart: 7, of which 1 were waited for; matrix products, arithmetic and copies ran while one was open for 0% of the time, Pallas kernels for 3%

profile of v5, /device:TPU:1, one launch (start us, length us, event | category | flops | bytes accessed | tf_op | source)
XLA Modules:
  0.0 101.7 jit_solution(14259578529571354070)
XLA Ops:
  0.6 1.3 %shard_map.143 = (f32[1,4,16384]{2,1,0:T(4,128)S(1)}, bf16[1,4,16384]{2,1,0:T(4,128)(2,1)S(1)}, f32[1,4,16384]{2,1,0:T(4,128)S(1)}, f32[1,4,16384]{2,1,0:T(4,128...) custom-call(f32[1,4,16384]{2,1,0:T(4,128)} %refs_0_.1, ...), custom_call_target="tpu_custom_call" | custom-call | tf_op jit(solution)/shard_map/pallas_call | solution.py:134
  1.9 28.3 %all_to_all.15.got_ref = f32[32,1,128]{2,1,0:T(1,128)S(1)} all-to-all(f32[32,1,128]{2,1,0:T(1,128)S(1)} %get-tuple-element.38), channel_id=1, replica_groups=mesh['zl'=4,'core'=2,'zh'=4,'y'=4,'x'=4] {'zh','zl','core'}, dimensions={0} | all-to-all | bytes 32768 | tf_op jit(solution)/shard_map/all_to_all | solution.py:121
  30.3 13.0 %all_to_all.16.refs_0_ = f32[16,1,128]{2,1,0:T(1,128)S(1)} all-to-all(f32[16,1,128]{2,1,0:T(1,128)S(1)} %shard_map.144), channel_id=1, replica_groups=mesh['zl'=4,'core'=2,'zh'=4,'y'=4,'x'=4] {'y','x'}, dimensions={0} | all-to-all | bytes 16384 | tf_op jit(solution)/shard_map/all_to_all | solution.py:121
  43.3 0.7 shard_map.145
  43.9 22.5 %all_to_all.17 = bf16[64,2,4,256]{3,2,1,0:T(4,128)(2,1)S(1)} all-to-all(bf16[64,2,4,256]{3,2,1,0:T(4,128)(2,1)S(1)} %get-tuple-element.47), channel_id=1, replica_groups=mesh['zl'=4,'core'=2,'zh'=4,'y'=4,'x'=4] {'zh','y','x'}, dimensions={0} | all-to-all | bytes 524288 | tf_op jit(solution)/shard_map/all_to_all | solution.py:121
  66.4 0.1 copy.18
  66.5 0.1 reshape.19.refs_0_
  66.6 7.0 %collective-permute-start.5 = (bf16[2,256,256]{2,1,0:T(8,128)(2,1)S(1)}, bf16[2,256,256]{2,1,0:T(8,128)(2,1)S(1)}, u32[]{:S(2)}, u32[]{:S(2)}) collective-permute-start(bf16[2,256,256]{2,1,0:T(8,128)(2,1)S(1)} %reshape.19.refs_0_), channel_id=1, source_target_pairs={{0,384},{128,256},{256,128},{384,0},{1,385},{129,257},{257,129},{3... | collective-permute-start | bytes 786440 | tf_op jit(solution)/shard_map/ppermute | solution.py:176
  73.6 3.2 %collective-permute-start.3 = (bf16[2,256,256]{2,1,0:T(8,128)(2,1)S(1)}, bf16[2,256,256]{2,1,0:T(8,128)(2,1)S(1)}, u32[]{:S(2)}, u32[]{:S(2)}) collective-permute-start(bf16[2,256,256]{2,1,0:T(8,128)(2,1)S(1)} %reshape.19.refs_0_), channel_id=1, source_target_pairs={{0,128},{128,0},{256,384},{384,256},{1,129},{129,1},{257,385},{385... | collective-permute-start | bytes 786440 | tf_op jit(solution)/shard_map/ppermute | solution.py:176
  76.8 1.9 %collective-permute-start = (bf16[2,256,256]{2,1,0:T(8,128)(2,1)S(1)}, bf16[2,256,256]{2,1,0:T(8,128)(2,1)S(1)}, u32[]{:S(2)}, u32[]{:S(2)}) collective-permute-start(bf16[2,256,256]{2,1,0:T(8,128)(2,1)S(1)} %reshape.19.refs_0_), channel_id=1, source_target_pairs={{0,256},{128,384},{256,0},{384,128},{1,257},{129,385},{257,1},{385... | collective-permute-start | bytes 786440 | tf_op jit(solution)/shard_map/ppermute | solution.py:176
  78.8 1.8 %shard_map.146 = (f32[1,4,16384]{2,1,0:T(4,128)}, f32[1,4,16384]{2,1,0:T(4,128)}, f32[1,4,16384]{2,1,0:T(4,128)}, f32[1,4,2048]{2,1,0:T(4,128)}, f32[1,4,2048]{2,1,0:T(4,128)}, /*index=5*/f32[1,4,2048]{2,1,0:T(4,128)}) custom-call(f32[1,1]{1,0:T(1,128)} %get-tuple-element.50.refs_0_, f32[1,4,16384]{2,1,0:T(4,128)S(1)} %get-tuple-element.39.refs_1_, ...), custom_call_target="tpu_custom_call" | custom-call | flops 1474560 | bytes 1916928 | tf_op jit(solution)/shard_map/pallas_call | solution.py:160
  80.5 6.3 %collective-permute-start.2 = (bf16[2,256,256]{2,1,0:T(8,128)(2,1)S(1)}, bf16[2,256,256]{2,1,0:T(8,128)(2,1)S(1)}, u32[]{:S(2)}, u32[]{:S(2)}) collective-permute-start(bf16[2,256,256]{2,1,0:T(8,128)(2,1)S(1)} %reshape.19.refs_0_), channel_id=1, source_target_pairs={{0,64},{64,0},{1,65},{65,1},{2,66},{66,2},{3,67},{67,3},{4,68},{68... | collective-permute-start | bytes 786440 | tf_op jit(solution)/shard_map/ppermute | solution.py:178
  86.8 0.0 collective-permute-done.5.refs_4_
  86.8 1.9 %collective-permute-start.6 = (bf16[2,256,256]{2,1,0:T(8,128)(2,1)S(1)}, bf16[2,256,256]{2,1,0:T(8,128)(2,1)S(1)}, u32[]{:S(2)}, u32[]{:S(2)}) collective-permute-start(bf16[2,256,256]{2,1,0:T(8,128)(2,1)S(1)} %collective-permute-done.5.refs_4_), channel_id=1, source_target_pairs={{0,64},{64,0},{1,65},{65,1},{2,66},{66,2},{3,67},{67,3},{4,68},{68... | collective-permute-start | bytes 786440 | tf_op jit(solution)/shard_map/ppermute | solution.py:178
  88.7 0.0 collective-permute-done.3.refs_2_
  88.7 2.4 %collective-permute-start.4 = (bf16[2,256,256]{2,1,0:T(8,128)(2,1)S(1)}, bf16[2,256,256]{2,1,0:T(8,128)(2,1)S(1)}, u32[]{:S(2)}, u32[]{:S(2)}) collective-permute-start(bf16[2,256,256]{2,1,0:T(8,128)(2,1)S(1)} %collective-permute-done.3.refs_2_), channel_id=1, source_target_pairs={{0,64},{64,0},{1,65},{65,1},{2,66},{66,2},{3,67},{67,3},{4,68},{68... | collective-permute-start | bytes 786440 | tf_op jit(solution)/shard_map/ppermute | solution.py:178
  91.2 4.1 %collective-permute-done.refs_0_ = bf16[2,256,256]{2,1,0:T(8,128)(2,1)S(1)} collective-permute-done((bf16[2,256,256]{2,1,0:T(8,128)(2,1)S(1)}, bf16[2,256,256]{2,1,0:T(8,128)(2,1)S(1)}, u32[]{:S(2)}, u32[]{:S(2)}) %collective-permute-start) | collective-permute-done | bytes 262176 | tf_op jit(solution)/shard_map/ppermute | solution.py:176
  95.3 4.3 %collective-permute-start.1 = (bf16[2,256,256]{2,1,0:T(8,128)(2,1)S(1)}, bf16[2,256,256]{2,1,0:T(8,128)(2,1)S(1)}, u32[]{:S(2)}, u32[]{:S(2)}) collective-permute-start(bf16[2,256,256]{2,1,0:T(8,128)(2,1)S(1)} %collective-permute-done.refs_0_), channel_id=1, source_target_pairs={{0,64},{64,0},{1,65},{65,1},{2,66},{66,2},{3,67},{67,3},{4,68},{68... | collective-permute-start | bytes 786440 | tf_op jit(solution)/shard_map/ppermute | solution.py:178
  99.6 0.0 collective-permute-done.2.refs_1_
  99.6 0.0 collective-permute-done.6.refs_5_
  99.6 0.0 collective-permute-done.4.refs_3_
  99.6 1.2 %shard_map.147 = (bf16[8,256,256]{2,1,0:T(8,128)(2,1)}, bf16[8,256,256]{2,1,0:T(8,128)(2,1)}) custom-call(bf16[2,256,256]{2,1,0:T(8,128)(2,1)S(1)} %reshape.19.refs_0_, bf16[2,256,256]{2,1,0:T(8,128)(2,1)S(1)} %collective-permute-done.2.refs_1_, bf16[2,256,256]{2,1,0:T(8,128)(2,1)S(1)} %collective-permute-done.3.refs_2_, ...), custom_call_target="tpu_custom_call" | custom-call | bytes 3145728 | tf_op jit(solution)/shard_map/pallas_call | solution.py:106
  100.9 0.0 collective-permute-done.1.refs_1_
  100.9 0.8 shard_map.148
  (1 shorter events, 0.0 us)
Async XLA Ops:
  66.6 20.2 %collective-permute-start.5 = (bf16[2,256,256]{2,1,0:T(8,128)(2,1)S(1)}, bf16[2,256,256]{2,1,0:T(8,128)(2,1)S(1)}, u32[]{:S(2)}, u32[]{:S(2)}) collective-permute-start(bf16[2,256,256]{2,1,0:T(8,128)(2,1)S(1)} %reshape.19.refs_0_), channel_id=1, source_target_pairs={{0,384},{128,256},{256,128},{384,0},{1,385},{129,257},{257,129},{3... | collective-permute-start | bytes 786440 | tf_op jit(solution)/shard_map/ppermute | solution.py:176
  73.6 15.2 %collective-permute-start.3 = (bf16[2,256,256]{2,1,0:T(8,128)(2,1)S(1)}, bf16[2,256,256]{2,1,0:T(8,128)(2,1)S(1)}, u32[]{:S(2)}, u32[]{:S(2)}) collective-permute-start(bf16[2,256,256]{2,1,0:T(8,128)(2,1)S(1)} %reshape.19.refs_0_), channel_id=1, source_target_pairs={{0,128},{128,0},{256,384},{384,256},{1,129},{129,1},{257,385},{385... | collective-permute-start | bytes 786440 | tf_op jit(solution)/shard_map/ppermute | solution.py:176
  76.8 18.4 %collective-permute-start = (bf16[2,256,256]{2,1,0:T(8,128)(2,1)S(1)}, bf16[2,256,256]{2,1,0:T(8,128)(2,1)S(1)}, u32[]{:S(2)}, u32[]{:S(2)}) collective-permute-start(bf16[2,256,256]{2,1,0:T(8,128)(2,1)S(1)} %reshape.19.refs_0_), channel_id=1, source_target_pairs={{0,256},{128,384},{256,0},{384,128},{1,257},{129,385},{257,1},{385... | collective-permute-start | bytes 786440 | tf_op jit(solution)/shard_map/ppermute | solution.py:176
  80.5 19.1 %collective-permute-start.2 = (bf16[2,256,256]{2,1,0:T(8,128)(2,1)S(1)}, bf16[2,256,256]{2,1,0:T(8,128)(2,1)S(1)}, u32[]{:S(2)}, u32[]{:S(2)}) collective-permute-start(bf16[2,256,256]{2,1,0:T(8,128)(2,1)S(1)} %reshape.19.refs_0_), channel_id=1, source_target_pairs={{0,64},{64,0},{1,65},{65,1},{2,66},{66,2},{3,67},{67,3},{4,68},{68... | collective-permute-start | bytes 786440 | tf_op jit(solution)/shard_map/ppermute | solution.py:178
  86.8 12.8 %collective-permute-start.6 = (bf16[2,256,256]{2,1,0:T(8,128)(2,1)S(1)}, bf16[2,256,256]{2,1,0:T(8,128)(2,1)S(1)}, u32[]{:S(2)}, u32[]{:S(2)}) collective-permute-start(bf16[2,256,256]{2,1,0:T(8,128)(2,1)S(1)} %collective-permute-done.5.refs_4_), channel_id=1, source_target_pairs={{0,64},{64,0},{1,65},{65,1},{2,66},{66,2},{3,67},{67,3},{4,68},{68... | collective-permute-start | bytes 786440 | tf_op jit(solution)/shard_map/ppermute | solution.py:178
  88.7 10.9 %collective-permute-start.4 = (bf16[2,256,256]{2,1,0:T(8,128)(2,1)S(1)}, bf16[2,256,256]{2,1,0:T(8,128)(2,1)S(1)}, u32[]{:S(2)}, u32[]{:S(2)}) collective-permute-start(bf16[2,256,256]{2,1,0:T(8,128)(2,1)S(1)} %collective-permute-done.3.refs_2_), channel_id=1, source_target_pairs={{0,64},{64,0},{1,65},{65,1},{2,66},{66,2},{3,67},{67,3},{4,68},{68... | collective-permute-start | bytes 786440 | tf_op jit(solution)/shard_map/ppermute | solution.py:178
  95.3 5.6 %collective-permute-start.1 = (bf16[2,256,256]{2,1,0:T(8,128)(2,1)S(1)}, bf16[2,256,256]{2,1,0:T(8,128)(2,1)S(1)}, u32[]{:S(2)}, u32[]{:S(2)}) collective-permute-start(bf16[2,256,256]{2,1,0:T(8,128)(2,1)S(1)} %collective-permute-done.refs_0_), channel_id=1, source_target_pairs={{0,64},{64,0},{1,65},{65,1},{2,66},{66,2},{3,67},{67,3},{4,68},{68... | collective-permute-start | bytes 786440 | tf_op jit(solution)/shard_map/ppermute | solution.py:178
